TPU v7x, 256 devices: a whole 4x4x8 slice. The times are simulated.
256 devices in a mesh: span: 8 (over x, y_hi), seq: 32 (over y_lo, z, core).
Axes of the slice: x: 4, y: 4 (y_hi: 2, y_lo: 2; y = y_hi * 2 + y_lo), z: 8, core: 2. Of those that a mesh axis runs over, the one named last changes fastest.
Arguments:
- hidden: bfloat16 [8, 1024, 3072], P('span', 'seq'), may hold values from -6 to 6
- levels: int32 [8], P('span'), may hold values from 0 to 15
- span_order: int32 [8], replicated, may hold values from 0 to 7, each once
- modulation: float32 [16, 3, 3072], replicated, may hold values from -1 to 4
- in_weight: bfloat16 [32, 3072, 384], P('seq'), may hold values from -1 to 1
- out_weight: bfloat16 [32, 128, 3072], P('seq'), may hold values from -0.109375 to 0.109375
- latent_weight: bfloat16 [3072, 64], replicated, may hold values from -0.109375 to 0.109375
- decoder_weight: bfloat16 [3, 3, 3, 16, 512], P(None, None, None, None, 'span'), may hold values from -0.3125 to 0.3125
Outputs:
- block_out: bfloat16 [8, 1024, 3072], P('span', 'seq')
- decoded: bfloat16 [32, 2, 64, 512], P('seq', None, None, 'span')
Inputs may be any that keep to these rules, and one draw needn't show every extreme that they name: `span_order`: each span has a different place in time.
All inputs are finite; a program needn't handle non-finite values.
Results may differ from a plain program's by a relative error of at most 0.03.
Values may be sent and summed in bfloat16 or wider, within the bound.
No kernel may reach another device: no remote copies, remote signals or barrier semaphores. Data moves between devices by JAX's collectives and lax.ppermute only.
A program may use at most 64 MiB of HBM per device.

v0:
```python
import math

import jax
import jax.numpy as jnp
from jax import lax
from jax.sharding import PartitionSpec as P

HEADS = 24
FR = 4
P_SIZE = 2
C = 16


EPSILON = 1e-06
NEG_LARGE = 1e30


def from_root(block, axis, owner):
    block = jnp.where(lax.axis_index(axis) == owner, block, jnp.zeros_like(block))
    return lax.psum(block, axis)


def with_halo(cells, sides, width):
    for axis, dim in sides:
        count = lax.axis_size(axis)
        head = lax.slice_in_dim(cells, 0, width, axis=dim)
        tail = lax.slice_in_dim(cells, cells.shape[dim] - width, cells.shape[dim], axis=dim)
        cells = jnp.concatenate(
            [
                lax.ppermute(tail, axis, [(i, (i + 1) % count) for i in range(count)]),
                cells,
                lax.ppermute(head, axis, [((i + 1) % count, i) for i in range(count)]),
            ],
            axis=dim,
        )
    return cells


def from_behind(block, axis, distance):
    devices = range(lax.axis_size(axis))
    route = [((i - distance) % len(devices), i) for i in devices]
    return lax.ppermute(block, axis, route)


def normalize(rows, shift_row, scale_row):
    values = rows.astype(jnp.float32)
    center = values - jnp.mean(values, axis=-1, keepdims=True)
    spread = jnp.mean(center * center, axis=-1, keepdims=True)
    return (center * lax.rsqrt(spread + EPSILON) * (1.0 + scale_row) + shift_row).astype(
        jnp.bfloat16
    )


def per_device(
    hidden, levels, span_order, modulation, in_weight, out_weight, latent_weight, decoder_weight
):
    head_slots = in_weight.shape[0]
    head_dim = in_weight.shape[2] // 3
    row_count = hidden.shape[1]
    mod_row = lax.dynamic_index_in_dim(modulation, levels[0], 0, keepdims=False)
    shift_row = mod_row[0]
    scale_row = mod_row[1]
    gate_row = mod_row[2]
    triples = jnp.einsum(
        "crd,hde->crhe",
        normalize(lax.all_gather(hidden, "seq", axis=1, tiled=True), shift_row, scale_row),
        in_weight,
        preferred_element_type=jnp.float32,
    ).astype(jnp.bfloat16)
    queries = triples[0, :, :, :head_dim]
    key_rows = triples[:, :, :, head_dim : 2 * head_dim]
    value_rows = triples[:, :, :, 2 * head_dim :]
    span_len = queries.shape[0]
    group_index = lax.axis_index("span")
    own_order = lax.dynamic_index_in_dim(span_order, group_index, 0, keepdims=False)
    my_rank = own_order.astype(jnp.float32)
    rank_tag = own_order.reshape(1, 1).astype(jnp.bfloat16)
    scale_factor = 1.0 / math.sqrt(head_dim)

    def attend(running, span_item):
        best_score, running_sum, accumulated = running
        key_block, value_block, rank_block = span_item
        scores = (
            jnp.einsum("qhd,khd->hqk", queries, key_block, preferred_element_type=jnp.float32)
            * scale_factor
        )
        visible = rank_block[0].astype(jnp.float32) <= my_rank
        block_best = jnp.where(visible, jnp.max(scores, axis=-1), -NEG_LARGE)
        new_best = jnp.maximum(best_score, block_best)
        factor = jnp.exp(best_score - new_best)
        weights = jnp.where(visible, jnp.exp(scores - new_best[:, :, None]), 0.0)
        running_sum = running_sum * factor + jnp.sum(weights, axis=-1)
        accumulated = accumulated * factor[:, :, None] + jnp.einsum(
            "hqk,khd->hqd",
            weights.astype(jnp.bfloat16),
            value_block,
            preferred_element_type=jnp.float32,
        )
        return ((new_best, running_sum, accumulated), None)

    start_state = (
        jnp.full((head_slots, span_len), -NEG_LARGE, jnp.float32),
        jnp.zeros((head_slots, span_len), jnp.float32),
        jnp.zeros((head_slots, span_len, head_dim), jnp.float32),
    )
    result, _ = lax.scan(
        attend,
        start_state,
        (
            lax.all_gather(key_rows, "span", axis=0, tiled=True),
            lax.all_gather(value_rows, "span", axis=0, tiled=True),
            lax.all_gather(rank_tag, "span", axis=0, tiled=True),
        ),
    )
    best_score, running_sum, accumulated = result
    attended = (accumulated / running_sum[:, :, None]).astype(jnp.bfloat16)
    slot_ids = lax.axis_index("seq") * head_slots + jnp.arange(head_slots, dtype=jnp.int32)
    attended = jnp.where((slot_ids < HEADS)[:, None, None], attended, jnp.zeros_like(attended))
    summed = lax.psum_scatter(
        jnp.einsum("hqd,hde->qe", attended, out_weight, preferred_element_type=jnp.float32).astype(
            jnp.bfloat16
        ),
        "seq",
        scatter_dimension=0,
        tiled=True,
    ).astype(jnp.float32)
    updated = (hidden[0].astype(jnp.float32) + gate_row * summed).astype(jnp.bfloat16)
    block_out = updated[None]
    latents = jnp.dot(updated, latent_weight, preferred_element_type=jnp.float32).astype(
        jnp.bfloat16
    )
    group_ids = jnp.arange(span_order.shape[0], dtype=jnp.int32)
    root_index = jnp.sum(jnp.where(span_order == 0, group_ids, 0))
    latents = from_root(latents, "span", root_index)
    slab = (
        latents.reshape(row_count, P_SIZE, P_SIZE, C)
        .transpose(1, 0, 2, 3)
        .reshape(P_SIZE, row_count * P_SIZE, C)
    )
    haloed = with_halo(slab, (("seq", 0),), 1)
    seq_count = lax.axis_size("seq")
    row_patches = seq_count // FR
    position = (lax.axis_index("seq") - row_patches // 2 + seq_count) % seq_count
    patch_row = position % row_patches
    frame_index = position // row_patches
    row_ids = jnp.arange(P_SIZE + 2, dtype=jnp.int32)
    keep = jnp.where(
        row_ids == 0,
        patch_row > 0,
        jnp.where(row_ids == P_SIZE + 1, patch_row < row_patches - 1, True),
    )
    haloed = jnp.where(keep[:, None, None], haloed, jnp.zeros_like(haloed))
    frames = [haloed]
    for frame_lag in (1, 2):
        earlier = from_behind(haloed, "seq", frame_lag * row_patches)
        frames.append(jnp.where(frame_index >= frame_lag, earlier, jnp.zeros_like(earlier)))
    width_cols = row_count * P_SIZE
    windows = []
    for time_off in range(3):
        framed = jnp.pad(frames[time_off], ((0, 0), (1, 1), (0, 0)))
        for row_off in range(3):
            for col_off in range(3):
                windows.append(framed[row_off : row_off + P_SIZE, col_off : col_off + width_cols])
    stacked = jnp.concatenate(windows, axis=-1).reshape(P_SIZE * width_cols, 27 * C)
    kernel = decoder_weight.reshape(27 * C, decoder_weight.shape[4])
    decoded = jnp.dot(stacked, kernel, preferred_element_type=jnp.float32).reshape(
        P_SIZE, width_cols, decoder_weight.shape[4]
    )
    return (block_out, decoded.astype(jnp.bfloat16)[None])


def solution(mesh):
    placed = (
        P("span", "seq", None),
        P("span"),
        P(),
        P(),
        P("seq", None, None),
        P("seq", None, None),
        P(),
        P(None, None, None, None, "span"),
    )
    return jax.shard_map(
        per_device,
        mesh=mesh,
        in_specs=placed,
        out_specs=(P("span", "seq", None), P("seq", None, None, "span")),
        check_vma=False,
    )
```

profile of v0, /device:TPU:10, one launch (start us, length us, event | category | flops | bytes accessed | tf_op | source)
XLA Modules:
  0.0 493.4 jit_solution(12321565084175282971)
XLA Ops:
  7.2 0.7 all-gather.5.cloned.1.call-update
  8.6 1.0 constant_dynamic-slice_fusion.1
  9.6 73.3 %all-gather.5.cloned.1.call-done = bf16[1,1024,3072]{2,1,0:T(8,128)(2,1)} async-done(((bf16[1,32,3072]{2,1,0:T(8,128)(2,1)}), bf16[1,1024,3072]{2,1,0:T(8,128)(2,1)}) %all-gather.5.cloned.1.call-update) | async-done | bytes 6291472 | tf_op jit(solution)/shard_map/all_gather | solution.py:66
  83.0 3.8 convert_reduce_fusion
  86.8 0.8 copy-done.2
  87.6 1.8 fusion.26
  89.4 3.6 fusion.39
  92.9 0.9 fusion.56
  93.9 0.7 all-gather.9.cloned.1.call-update
  94.7 0.6 dynamic_slice.20
  95.9 0.6 dynamic-slice
  96.5 0.8 dynamic-update-slice
  97.3 21.3 %all-reduce.3 = bf16[8]{0:T(256)(128)(2,1)S(1)} all-reduce(bf16[8]{0:T(256)(128)(2,1)S(1)} %dynamic-update-slice), channel_id=2, replica_groups=mesh['span'=8,'seq'=32] {'span'}, use_global_device_ids=true, to_apply=%add.3 | all-reduce | flops 8 | bytes 32
  119.3 33.6 %all-gather.7.cloned.1.call-done = bf16[8,1024,1,128]{3,1,2,0:T(8,128)(2,1)} async-done(((bf16[1,1024,1,128]{3,1,2,0:T(8,128)(2,1)}), bf16[8,1024,1,128]{3,1,2,0:T(8,128)(2,1)}) %all-gather.7.cloned.1.call-update) | async-done | bytes 2097168 | tf_op jit(solution)/shard_map/all_gather | solution.py:110
  152.9 61.6 %all-gather.9.cloned.1.call-done = bf16[8,1024,1,128]{3,1,2,0:T(8,128)(2,1)} async-done(((bf16[1,1024,1,128]{3,1,2,0:T(8,128)(2,1)}), bf16[8,1024,1,128]{3,1,2,0:T(8,128)(2,1)}) %all-gather.9.cloned.1.call-update) | async-done | bytes 2097168 | tf_op jit(solution)/shard_map/all_gather | solution.py:111
  214.5 83.4 %while.15 = (s32[]{:T(128)}, f32[1,1024]{1,0:T(1,128)S(1)}, f32[1,1024]{1,0:T(1,128)S(1)}, f32[1,1024,128]{2,1,0:T(8,128)S(1)}, bf16[8,1]{0,1:T(2,128)(2,1)S(1)}...) while((s32[]{:T(128)}, f32[1,1024]{1,0:T(1,128)S(1)}, ...), condition=%wide.region_5.6_spmd.clone, body=%wide.region_2.5_spmd.clone.sunk | while | flops 547756032 | bytes 31270056 | solution.py:106
  214.5 0.6 constant_dynamic-slice_fusion.4
  215.7 3.6 multiply_reduce_fusion.2
  219.3 3.2 fusion.70
  222.6 0.2 copy-done.1
  222.8 2.1 fusion.72
  224.9 0.6 constant_dynamic-slice_fusion.4
  226.2 3.6 multiply_reduce_fusion.2
  229.8 3.2 fusion.70
  233.0 0.2 copy-done.1
  233.2 2.1 fusion.72
  235.3 0.6 constant_dynamic-slice_fusion.4
  236.6 3.6 multiply_reduce_fusion.2
  240.2 3.2 fusion.70
  243.7 2.1 fusion.72
  245.7 0.6 constant_dynamic-slice_fusion.4
  247.0 3.6 multiply_reduce_fusion.2
  250.7 3.2 fusion.70
  253.9 0.2 copy-done.1
  254.1 2.1 fusion.72
  256.2 0.6 constant_dynamic-slice_fusion.4
  257.5 3.6 multiply_reduce_fusion.2
  261.1 3.2 fusion.70
  264.3 0.2 copy-done.1
  264.5 2.1 fusion.72
  266.6 0.6 constant_dynamic-slice_fusion.4
  267.9 3.6 multiply_reduce_fusion.2
  271.5 3.2 fusion.70
  275.0 2.1 fusion.72
  277.1 0.6 constant_dynamic-slice_fusion.4
  278.3 3.6 multiply_reduce_fusion.2
  282.0 3.2 fusion.70
  285.4 2.1 fusion.72
  287.5 0.6 constant_dynamic-slice_fusion.4
  288.8 3.6 multiply_reduce_fusion.2
  292.4 3.2 fusion.70
  295.8 2.1 fusion.72
  297.9 5.7 %convolution_convert_fusion = bf16[1024,3072]{1,0:T(8,128)(2,1)} fusion(bf16[1,128,3072]{2,1,0:T(8,128)(2,1)} %param.15, f32[1,1024,128]{2,1,0:T(8,128)S(1)} %get-tuple-element.50, f32[1024]{0:T(1024)S(1)} %bitcast.102, pred[]{:T(512)S(6)} %lt.29), kind=kOutput, calls=%fused_computation.37 | convolution fusion | flops 808845312 | bytes 7606273 | tf_op jit(solution)/shard_map/hqd,hde->qe/dot_general | solution.py:120
  303.6 0.6 fusion.54
  305.0 123.5 %reduce-scatter.2.cloned.1.call-done = bf16[32,3072]{1,0:T(8,128)(2,1)} async-done(((bf16[1024,3072]{1,0:T(8,128)(2,1)}), bf16[32,3072]{1,0:T(8,128)(2,1)}) %reduce-scatter.2.cloned.1.call-update) | async-done | bytes 196624 | tf_op jit(solution)/shard_map/reduce_scatter | solution.py:119
  428.5 1.2 fusion.45
  429.8 38.9 %psum.7 = bf16[2,32,2,16]{1,3,2,0:T(8,128)(2,1)S(1)} all-reduce(bf16[2,32,2,16]{1,3,2,0:T(8,128)(2,1)S(1)} %bitcast.108), channel_id=1, replica_groups=mesh['span'=8,'seq'=32] {'span'}, use_global_device_ids=true, to_apply=%region_8.9 | all-reduce | flops 2048 | bytes 8192 | tf_op jit(solution)/shard_map/psum | solution.py:20
  468.9 3.9 collective-permute-start.1
  472.9 1.7 fusion.53
  474.7 1.9 collective-permute-start.3
  476.6 2.4 collective-permute-done.3
  479.1 6.5 %collective-permute-done.2 = bf16[4,64,16]{2,1,0:T(8,128)(2,1)S(1)} collective-permute-done((bf16[4,64,16]{2,1,0:T(8,128)(2,1)S(1)}, bf16[4,64,16]{2,1,0:T(8,128)(2,1)S(1)}, u32[]{:S(2)}, u32[]{:S(2)}) %collective-permute-start.2) | collective-permute-done | bytes 8224 | tf_op jit(solution)/shard_map/ppermute | solution.py:42
  485.7 0.3 concatenate.7
  486.1 0.8 fusion.44
  (85 shorter events, 2.1 us)
Async XLA Ops:
  7.2 82.2 %copy-start = (bf16[1,3072,384]{2,1,0:T(8,128)(2,1)S(1)}, bf16[1,3072,384]{2,1,0:T(8,128)(2,1)}, u32[]{:S(2)}) copy-start(bf16[1,3072,384]{2,1,0:T(8,128)(2,1)} %param.14) | copy-start | bytes 7077892
  7.2 75.8 %all-gather.5.cloned.1.call-start = ((), (), s32[]{:S(2)}) async-start(), calls=%async_computation.1 | async-start | bytes 6488064 | tf_op jit(solution)/shard_map/all_gather | solution.py:66
  7.9 144.9 %all-gather.7.cloned.1.call-start = ((), (), s32[]{:S(2)}) async-start(), calls=%async_computation.2 | async-start | bytes 2359296 | tf_op jit(solution)/shard_map/all_gather | solution.py:110
  83.0 4.6 copy-start.2
  89.3 5.3 %copy-start.6 = (s32[8]{0:T(128)S(1)}, s32[8]{0:T(128)}, u32[]{:S(2)}) copy-start(s32[8]{0:T(128)} %param.12) | copy-start | bytes 100
  89.3 6.6 %copy-start.7 = (u32[256]{0:T(256)S(1)}, u32[256]{0:T(256)}, u32[]{:S(2)}) copy-start(u32[256]{0:T(256)} %constant.120) | copy-start | bytes 3076
  93.9 120.6 %all-gather.9.cloned.1.call-start = ((), (), s32[]{:S(2)}) async-start(), calls=%async_computation.3 | async-start | bytes 2359296 | tf_op jit(solution)/shard_map/all_gather | solution.py:111
  94.6 333.9 %reduce-scatter.2.cloned.1.call-start = ((), (), s32[]{:S(2)}) async-start(), calls=%async_computation.4 | async-start | bytes 6488064 | tf_op jit(solution)/shard_map/reduce_scatter | solution.py:119
  219.3 3.4 copy-start.1
  229.8 3.4 copy-start.1
  240.2 3.4 copy-start.1
  250.6 3.4 copy-start.1
  261.1 3.4 copy-start.1
  271.5 3.4 copy-start.1
  281.9 3.4 copy-start.1
  292.4 3.4 copy-start.1
  303.6 124.9 %copy-start.3 = (bf16[1,32,3072]{2,1,0:T(8,128)(2,1)S(1)}, bf16[1,32,3072]{2,1,0:T(8,128)(2,1)}, u32[]{:S(2)}) copy-start(bf16[1,32,3072]{2,1,0:T(8,128)(2,1)} %param.10) | copy-start | bytes 589828
  303.6 124.9 %copy-start.4 = (bf16[3072,64]{0,1:T(8,128)(2,1)S(1)}, bf16[3072,64]{0,1:T(8,128)(2,1)}, u32[]{:S(2)}) copy-start(bf16[3072,64]{0,1:T(8,128)(2,1)} %param.16) | copy-start | bytes 1179652
  303.6 182.5 %copy-start.5 = (bf16[3,3,3,16,64]{4,3,2,1,0:T(8,128)(2,1)S(1)}, bf16[3,3,3,16,64]{4,3,2,1,0:T(8,128)(2,1)}, u32[]{:S(2)}) copy-start(bf16[3,3,3,16,64]{4,3,2,1,0:T(8,128)(2,1)} %param.17) | copy-start | bytes 165892
  468.8 5.9 %collective-permute-start = (bf16[1,64,16]{2,1,0:T(8,128)(2,1)S(1)}, bf16[1,64,16]{2,1,0:T(8,128)(2,1)S(1)}, u32[]{:S(2)}, u32[]{:S(2)}) collective-permute-start(bf16[1,64,16]{2,1,0:T(8,128)(2,1)S(1)} %bitcast.109), channel_id=1, source_target_pairs={{0,1},{1,2},{2,3},{3,4},{4,5},{5,6},{6,7},{7,8},{8,9},{9,10},{10,1... | collective-permute-start | bytes 6152 | tf_op jit(solution)/shard_map/ppermute | solution.py:30
  468.9 5.7 %collective-permute-start.1 = (bf16[1,64,16]{2,1,0:T(8,128)(2,1)S(1)}, bf16[1,64,16]{2,1,0:T(8,128)(2,1)S(1)}, u32[]{:S(2)}, u32[]{:S(2)}) collective-permute-start(bf16[1,64,16]{2,1,0:T(8,128)(2,1)S(1)} %bitcast.110), channel_id=1, source_target_pairs={{1,0},{2,1},{3,2},{4,3},{5,4},{6,5},{7,6},{8,7},{9,8},{10,9},{11,1... | collective-permute-start | bytes 6152 | tf_op jit(solution)/shard_map/ppermute | solution.py:32
  474.7 4.3 collective-permute-start.3
  476.6 9.1 %collective-permute-start.2 = (bf16[4,64,16]{2,1,0:T(8,128)(2,1)S(1)}, bf16[4,64,16]{2,1,0:T(8,128)(2,1)S(1)}, u32[]{:S(2)}, u32[]{:S(2)}) collective-permute-start(bf16[4,64,16]{2,1,0:T(8,128)(2,1)S(1)} %maximum_select_fusion), channel_id=1, source_target_pairs={{24,0},{25,1},{26,2},{27,3},{28,4},{29,5},{30,6},{31,7},{0,8},{1,9... | collective-permute-start | bytes 24584 | tf_op jit(solution)/shard_map/ppermute | solution.py:42
Sparse Core Ops, SparseCore 0:
  9.9 73.0 all-gather.4
  94.0 58.8 all-gather.6
  155.5 58.9 all-gather.8
  303.7 124.7 reduce-scatter.1
where the time goes:
time: 496 us; the launch traced here: 493 us
  waiting for transfers between devices  302 us (61%)
  blocking collectives  60.2 us (12%)
  matrix products  56.6 us (11%)
  other arithmetic  34.9 us (7%)
  between operations  16.7 us (3%)
  local copies, waits for them, and re-layouts  11.4 us (2%)
  starting transfers between devices  6.01 us (1%)
  loops' own time  5.34 us (1%)
    reduce_scatter x1, waiting for transfers between devices, per_device(): lax.psum_scatter(jnp.einsum('hqd,hde->qe', attended, out_weight, preferre...  124 us
    all_gather x1, waiting for transfers between devices, per_device(): lax.all_gather(hidden, 'seq', axis=1, tiled=True)  73.3 us
    all_gather x1, waiting for transfers between devices, per_device(): lax.all_gather(value_rows, 'span', axis=0, tiled=True)  61.6 us
    psum x1, blocking collectives, from_root(): return lax.psum(block, axis)  38.9 us
    all_gather x1, waiting for transfers between devices, per_device(): lax.all_gather(key_rows, 'span', axis=0, tiled=True)  33.6 us
    dot_general x8, matrix products, attend(): jnp.einsum('qhd,khd->hqk', queries, key_block, preferred_element_type=jnp...  28.9 us
    reduce_sum x8, other arithmetic, attend(): running_sum = running_sum * factor + jnp.sum(weights, axis=-1)  25.6 us
    unnamed x1, blocking collectives  21.3 us
  transfers between devices with their start and end apart: 8, of which 6 were waited for; matrix products, arithmetic and copies ran while one was open for 1% of the time, Pallas kernels for 0%

commit v1 on v0

v1 whole, which is shorter than its diff:
```python
import functools
import math

import jax
import jax.numpy as jnp
from jax import lax
from jax.experimental import pallas as pl
from jax.experimental.pallas import tpu as pltpu
from jax.sharding import PartitionSpec as P

HEADS = 24
FR = 4
P_SIZE = 2
C = 16
HD = 128

EPSILON = 1e-06
NEG_LARGE = 1e30

NX, NH, NY, NZ, NC = 4, 2, 2, 8, 2
BLK = 32
QUARTER = NZ * BLK
TAIL = 16


def seq_at(y, z, c):
    return ((y % NY) * NZ + z % NZ) * NC + c % NC


def span_at(x, h):
    return (x % NX) * NH + h % NH


def seq_route(dy=0, dz=0, dc=0):
    return [
        (seq_at(y, z, c), seq_at(y + dy, z + dz, c + dc))
        for y in range(NY)
        for z in range(NZ)
        for c in range(NC)
    ]


def span_route(dx=0, dh=0):
    return [(span_at(x, h), span_at(x + dx, h + dh)) for x in range(NX) for h in range(NH)]


def move_z(a, d):
    return lax.ppermute(a, "seq", seq_route(dz=d))


def move_y(a):
    return lax.ppermute(a, "seq", seq_route(dy=1))


def move_core(a):
    return lax.ppermute(a, "seq", seq_route(dc=1))


def move_x(a, d):
    return lax.ppermute(a, "span", span_route(dx=d))


def move_hi(a):
    return lax.ppermute(a, "span", span_route(dh=1))


def normalize(rows, shift_row, scale_row):
    values = rows.astype(jnp.float32)
    center = values - jnp.mean(values, axis=-1, keepdims=True)
    spread = jnp.mean(center * center, axis=-1, keepdims=True)
    return (center * lax.rsqrt(spread + EPSILON) * (1.0 + scale_row) + shift_row).astype(
        jnp.bfloat16
    )


def gather_class(b):
    n = b.shape[0] // 2
    up1, dn1, y0 = move_z(b, 1), move_z(b, -1), move_y(b)
    up2, dn2 = move_z(up1, 1), move_z(dn1, -1)
    yu1, yd1 = move_y(up1), move_y(dn1)
    up3, dn3 = move_z(up2, 1), move_z(dn2, -1)
    yu2, yd2 = move_y(up2), move_y(dn2)
    f4a, f4b = move_z(up3[:n], 1), move_z(dn3[n:], -1)
    yu3, yd3 = move_z(yu2, 1), move_z(yd2, -1)
    y4a, y4b = move_z(yu3[:n], 1), move_z(yd3[n:], -1)
    mine = [b, dn1, dn2, dn3, f4a, f4b, up3, up2, up1]
    other = [y0, yd1, yd2, yd3, y4a, y4b, yu3, yu2, yu1]
    return jnp.concatenate(mine + other, axis=0)


def dot_t(a, b):
    return lax.dot_general(a, b, (((1,), (1,)), ((), ())), preferred_element_type=jnp.float32)


EXP_SCALE = math.log2(math.e) / math.sqrt(HD)


def self_kernel(q_ref, kv_ref, o_ref):
    s = dot_t(q_ref[...], kv_ref[:, :HD])
    m = jnp.max(s, axis=1, keepdims=True)
    p = jnp.exp2((s - m) * EXP_SCALE)
    total = jnp.sum(p, axis=1, keepdims=True)
    acc = jnp.dot(p.astype(jnp.bfloat16), kv_ref[:, HD:], preferred_element_type=jnp.float32)
    o_ref[...] = (acc / total).astype(jnp.bfloat16)


def self_attention(q, kv):
    rows = q.shape[0]
    return pl.pallas_call(
        self_kernel,
        grid=(rows // QUARTER,),
        in_specs=[
            pl.BlockSpec((QUARTER, HD), lambda i: (i, 0)),
            pl.BlockSpec(kv.shape, lambda i: (0, 0)),
        ],
        out_specs=pl.BlockSpec((QUARTER, HD), lambda i: (i, 0)),
        out_shape=jax.ShapeDtypeStruct((rows, HD), jnp.bfloat16),
        compiler_params=pltpu.CompilerParams(vmem_limit_bytes=32 * 2**20),
        name="self_attention",
    )(q, kv)


def main_kernel(s_ref, qa_ref, qb_ref, k0, k1, k2, k3a, k3b, o_ref, acc, m_s, l_s):
    r = pl.program_id(0)
    dh = r // 4
    q = jnp.where(dh == 0, qa_ref[...], qb_ref[...])
    acc[...] = jnp.zeros_like(acc)
    m_s[...] = jnp.full_like(m_s, -NEG_LARGE)
    l_s[...] = jnp.zeros_like(l_s)

    def update(refs):
        ss = [dot_t(q, ref[:, :HD]) for ref in refs]
        m_old = m_s[:, :1]
        m_new = m_old
        for s in ss:
            m_new = jnp.maximum(m_new, jnp.max(s, axis=1, keepdims=True))
        alpha = jnp.exp2((m_old - m_new) * EXP_SCALE)
        total = l_s[:, :1] * alpha
        out = acc[...] * alpha
        for s, ref in zip(ss, refs):
            p = jnp.exp2((s - m_new) * EXP_SCALE)
            total = total + jnp.sum(p, axis=1, keepdims=True)
            out = out + jnp.dot(
                p.astype(jnp.bfloat16), ref[:, HD:], preferred_element_type=jnp.float32
            )
        acc[...] = out
        m_s[...] = jnp.broadcast_to(m_new, m_s.shape)
        l_s[...] = jnp.broadcast_to(total, l_s.shape)

    for i, refs in enumerate(((k0,), (k1,), (k2,), (k3a, k3b))):
        pl.when(s_ref[dh * 4 + i] == 1)(functools.partial(update, refs))

    total = l_s[...]
    some = total > 0.0
    safe = jnp.where(some, total, 1.0)
    o_ref[0, :QUARTER, :] = (acc[...] / safe).astype(jnp.bfloat16)
    lse = jnp.where(some, m_s[...] * EXP_SCALE + jnp.log2(safe), -NEG_LARGE)
    row = lse.T[0:1, :]
    row = jnp.concatenate([row[:, :128], row[:, 128:]], axis=0)
    hi = row.astype(jnp.bfloat16).astype(jnp.float32)
    rest = row - hi
    mid = rest.astype(jnp.bfloat16).astype(jnp.float32)
    low = rest - mid
    pad = jnp.zeros((TAIL - 6, 128), jnp.float32)
    o_ref[0, QUARTER:, :] = jnp.concatenate([hi, mid, low, pad], axis=0).astype(jnp.bfloat16)


def main_attention(flags, place, qa, qb, blocks):
    scalars = jnp.concatenate([flags, place.reshape(1)])
    whole = [pl.BlockSpec(b.shape, lambda r, s: (0, 0)) for b in blocks]
    return pl.pallas_call(
        main_kernel,
        grid_spec=pltpu.PrefetchScalarGridSpec(
            num_scalar_prefetch=1,
            grid=(8,),
            in_specs=[
                pl.BlockSpec((QUARTER, HD), lambda r, s: (r % 4, 0)),
                pl.BlockSpec((QUARTER, HD), lambda r, s: (r % 4, 0)),
            ]
            + whole,
            out_specs=pl.BlockSpec((1, QUARTER + TAIL, HD), lambda r, s: (r ^ s[8], 0, 0)),
            scratch_shapes=[
                pltpu.VMEM((QUARTER, HD), jnp.float32),
                pltpu.VMEM((QUARTER, 128), jnp.float32),
                pltpu.VMEM((QUARTER, 128), jnp.float32),
            ],
        ),
        out_shape=jax.ShapeDtypeStruct((8, QUARTER + TAIL, HD), jnp.bfloat16),
        compiler_params=pltpu.CompilerParams(vmem_limit_bytes=32 * 2**20),
        name="main_attention",
    )(scalars, qa, qb, *blocks)


def join_kernel(s_ref, in_ref, a_ref):
    place = s_ref[0]
    z = s_ref[1]
    for r in range(4):
        parts = []
        for dh in range(2):
            at = (dh * 4 + r) ^ place
            rows = in_ref[at, QUARTER:, :].astype(jnp.float32)
            parts.append((at, rows[0:2] + rows[2:4] + rows[4:6]))
        top = jnp.maximum(parts[0][1], parts[1][1])
        e = [jnp.exp2(lse - top) for _, lse in parts]
        norm = e[0] + e[1]
        for half in range(2):
            out = None
            for (at, _), weight in zip(parts, e):
                w = (weight / norm)[half : half + 1, :]
                col = jnp.broadcast_to(w, (128, 128)).T
                term = in_ref[at, half * 128 : half * 128 + 128, :].astype(jnp.float32) * col
                out = term if out is None else out + term
            out = out.astype(jnp.bfloat16)
            slot = (r % 2) * 2 + r // 2
            for j in range(4):
                d = half * 4 + j
                start = pl.multiple_of(((z + d) % NZ) * BLK, BLK)
                a_ref[pl.ds(start, BLK), slot * HD : slot * HD + HD] = out[j * BLK : j * BLK + BLK]


def join_heads(place, z, received):
    return pl.pallas_call(
        join_kernel,
        grid_spec=pltpu.PrefetchScalarGridSpec(
            num_scalar_prefetch=1,
            grid=(1,),
            in_specs=[pl.BlockSpec(received.shape, lambda i, s: (0, 0, 0))],
            out_specs=pl.BlockSpec((QUARTER, 4 * HD), lambda i, s: (0, 0)),
        ),
        out_shape=jax.ShapeDtypeStruct((QUARTER, 4 * HD), jnp.bfloat16),
        name="join_heads",
    )(jnp.stack([place, z]), received)


def decode(latents, root_kernel):
    seq_count = latents.shape[0]
    row_patches = seq_count // FR
    me = lax.axis_index("seq")
    ringed = jnp.concatenate([latents[-1:], latents, latents[:1]], axis=0)
    position = (me - row_patches // 2 + seq_count) % seq_count
    patch_row = position % row_patches
    frame_index = position // row_patches
    row_ids = jnp.arange(P_SIZE + 2, dtype=jnp.int32)
    keep = jnp.where(
        row_ids == 0,
        patch_row > 0,
        jnp.where(row_ids == P_SIZE + 1, patch_row < row_patches - 1, True),
    )
    width_cols = BLK * P_SIZE
    windows = []
    for lag in range(3):
        start = (me - lag * row_patches + seq_count) % seq_count
        three = lax.dynamic_slice_in_dim(ringed, start, 3, axis=0)
        slab = (
            three.reshape(3, BLK, P_SIZE, P_SIZE, C)
            .transpose(0, 2, 1, 3, 4)
            .reshape(3 * P_SIZE, width_cols, C)
        )[P_SIZE - 1 : 2 * P_SIZE + 1]
        ok = keep & (frame_index >= lag)
        slab = jnp.where(ok[:, None, None], slab, jnp.zeros_like(slab))
        framed = jnp.pad(slab, ((0, 0), (1, 1), (0, 0)))
        for row_off in range(3):
            for col_off in range(3):
                windows.append(framed[row_off : row_off + P_SIZE, col_off : col_off + width_cols])
    stacked = jnp.concatenate(windows, axis=-1).reshape(P_SIZE * width_cols, 27 * C)
    decoded = jnp.dot(stacked, root_kernel, preferred_element_type=jnp.float32)
    return decoded.reshape(P_SIZE, width_cols, root_kernel.shape[1]).astype(jnp.bfloat16)[None]


def per_device(
    hidden, levels, span_order, modulation, in_weight, out_weight, latent_weight, decoder_weight
):
    span_me = lax.axis_index("span")
    seq_me = lax.axis_index("seq")
    x, h = span_me // NH, span_me % NH
    y, z, core = seq_me // (NZ * NC), (seq_me // NC) % NZ, seq_me % NC
    mod_row = lax.dynamic_index_in_dim(modulation, levels[0], 0, keepdims=False)
    shift_row, scale_row, gate_row = mod_row[0], mod_row[1], mod_row[2]

    w_own = in_weight[0]
    w_oth = move_core(w_own)
    out_w = jnp.where(seq_me < HEADS, out_weight[0], jnp.zeros_like(out_weight[0]))

    rows = gather_class(normalize(hidden[0], shift_row, scale_row))
    mine = jnp.dot(rows, w_own, preferred_element_type=jnp.float32).astype(jnp.bfloat16)
    theirs = jnp.dot(rows, w_oth, preferred_element_type=jnp.float32).astype(jnp.bfloat16)
    triples = jnp.concatenate([mine, move_core(theirs)], axis=0)
    q = triples[:, :HD]
    kv = triples[:, HD:]

    q_hi = move_hi(q)
    half = kv.shape[0] // 2
    kv_up, kv_dn = move_x(kv, 1), move_x(kv, -1)
    kv_2a, kv_2b = move_x(kv_up[:half], 1), move_x(kv_dn[half:], -1)

    pair = jnp.concatenate([out_w, move_core(out_w)], axis=0)
    far_pair = move_y(lax.optimization_barrier((pair, rows))[0])

    own = self_attention(q, kv)
    gated = out_w.astype(jnp.float32) * gate_row
    head_latent = jnp.dot(
        gated, latent_weight.astype(jnp.float32), precision=lax.Precision.HIGHEST
    )
    part = jnp.dot(own.astype(jnp.float32), head_latent, precision=lax.Precision.HIGHEST)
    pv = latent_weight.shape[1]
    part = part.astype(jnp.bfloat16).reshape(NC, NY, NZ, BLK, pv)
    part = jnp.where(core == 1, part[::-1], part)
    part = jnp.where(y == 1, part[:, ::-1], part)
    twice = jnp.concatenate([part, part], axis=2)
    part = lax.dynamic_slice_in_dim(twice, (NZ - z) % NZ, NZ, axis=2)
    part = part.transpose(1, 2, 0, 3, 4).reshape(NY * NZ * NC, BLK, pv)
    part = lax.all_to_all(part, "seq", 0, 0, tiled=True)
    latents = jnp.sum(part.astype(jnp.float32), axis=0) + jnp.dot(
        hidden[0], latent_weight, preferred_element_type=jnp.float32
    )
    latents = latents.astype(jnp.bfloat16)
    group_ids = jnp.arange(span_order.shape[0], dtype=jnp.int32)
    root = jnp.sum(jnp.where(span_order == 0, group_ids, 0))
    spread = lax.all_to_all(
        jnp.broadcast_to(latents[None], (NX * NH, BLK, pv)), "span", 0, 0, tiled=True
    )
    latents = lax.dynamic_index_in_dim(spread, root, 0, keepdims=True)
    every = lax.all_to_all(
        jnp.broadcast_to(latents, (NY * NZ * NC, BLK, pv)), "seq", 0, 0, tiled=True
    )
    decoded = decode(every, decoder_weight.reshape(27 * C, decoder_weight.shape[4]))

    order_of = lambda dx, dh: span_order[((x + dx) % NX) * NH + (h + dh) % NH]
    seen = [order_of(d, 0) for d in (0, -1, 1, 2)]
    flags = jnp.stack([(s <= order_of(0, dh)).astype(jnp.int32) for dh in range(2) for s in seen])
    place = h * 4 + core * 2 + y
    chunks = main_attention(flags, place, q, q_hi, (kv, kv_up, kv_dn, kv_2a, kv_2b))
    groups = [
        [
            span_at(i, hh) * (NY * NZ * NC) + seq_at(yy, j, cc)
            for hh in range(NH)
            for cc in range(NC)
            for yy in range(NY)
        ]
        for i in range(NX)
        for j in range(NZ)
    ]
    received = lax.all_to_all(
        chunks, ("span", "seq"), 0, 0, tiled=True, axis_index_groups=groups
    )
    heads = join_heads(place, z, received)
    partial = jnp.dot(heads[:, : 2 * HD], pair, preferred_element_type=jnp.float32) + jnp.dot(
        heads[:, 2 * HD :], far_pair, preferred_element_type=jnp.float32
    )
    z_groups = [[seq_at(yy, j, cc) for j in range(NZ)] for yy in range(NY) for cc in range(NC)]
    summed = lax.psum_scatter(
        partial.astype(jnp.bfloat16),
        "seq",
        scatter_dimension=0,
        tiled=True,
        axis_index_groups=z_groups,
    ).astype(jnp.float32)
    block_out = (hidden[0].astype(jnp.float32) + gate_row * summed).astype(jnp.bfloat16)[None]
    return (block_out, decoded)


def solution(mesh):
    placed = (
        P("span", "seq", None),
        P("span"),
        P(),
        P(),
        P("seq", None, None),
        P("seq", None, None),
        P(),
        P(None, None, None, None, "span"),
    )
    return jax.shard_map(
        per_device,
        mesh=mesh,
        in_specs=placed,
        out_specs=(P("span", "seq", None), P("seq", None, None, "span")),
        check_vma=False,
    )
```

time: 496 us -> 220 us (0.44)
  waiting for transfers between devices: 302 us -> 58.3 us
  starting transfers between devices: 6.01 us -> 60.9 us
  blocking collectives: 60.2 us -> 15.2 us
  matrix products: 56.6 us -> 13.6 us
  other arithmetic: 34.9 us -> 11.2 us
  Pallas kernels: 0 us -> 17.3 us
  between operations: 16.7 us -> 26 us
  loops' own time: 5.34 us -> 0 us
    all_gather x3 -> x0, waiting for transfers between devices: 168 us -> none  [the longest x1 73.3 us: per_device(): lax.all_gather(hidden, 'seq', axis=1, tiled=True)]
    reduce_scatter x1, waiting for transfers between devices: 124 us -> 0.01 us  [per_device(): lax.psum_scatter(partial.astype(jnp.bfloat16), 'seq', scatter_dimension=0...]
    dot_general x20 -> x8, matrix products: 56.6 us -> 13.6 us  [the longest x1 3.62 us: per_device(): jnp.dot(rows, w_oth, preferred_element_type=jnp.float32)]
    psum x1 -> x0, blocking collectives: 38.9 us -> none  [from_root(): return lax.psum(block, axis)]
    all_to_all x0 -> x3, starting transfers between devices: none -> 30.3 us  [the longest x1 17.8 us: per_device(): lax.all_to_all(chunks, ('span', 'seq'), 0, 0, tiled=True, axis_index_grou...]
    ppermute x4 -> x26, waiting for transfers between devices: 8.96 us -> 37.1 us  [the longest x12 26.4 us: move_z(): return lax.ppermute(a, 'seq', seq_route(dz=d))]
    reduce_sum x9 -> x2, other arithmetic: 26.2 us -> 0.7 us  [the longest x1 0.63 us: per_device(): root = jnp.sum(jnp.where(span_order == 0, group_ids, 0))]
    ppermute x4 -> x26, starting transfers between devices: 5.85 us -> 30.6 us  [the longest x12 18.2 us: move_z(): return lax.ppermute(a, 'seq', seq_route(dz=d))]
  transfers between devices with their start and end apart: 8 -> 30, of which waited for: 6 -> 12; matrix products, arithmetic and copies ran while one was open for 1% -> 13% of each run, Pallas kernels for 0% -> 8%
where the time goes in v1:
time: 220 us; the launch traced here: 216 us
  starting transfers between devices  60.9 us (28%)
  waiting for transfers between devices  58.3 us (26%)
  between operations  26 us (12%)
  Pallas kernels  17.3 us (8%)
  blocking collectives  15.2 us (7%)
  local copies, waits for them, and re-layouts  13.7 us (6%)
  matrix products  13.6 us (6%)
  other arithmetic  11.2 us (5%)
    ppermute x12, waiting for transfers between devices, move_z(): return lax.ppermute(a, 'seq', seq_route(dz=d))  26.4 us
    ppermute x12, starting transfers between devices, move_z(): return lax.ppermute(a, 'seq', seq_route(dz=d))  18.2 us
    all_to_all x1, starting transfers between devices, per_device(): lax.all_to_all(chunks, ('span', 'seq'), 0, 0, tiled=True, axis_index_grou...  17.8 us
    all_to_all x1, blocking collectives, per_device(): part = lax.all_to_all(part, 'seq', 0, 0, tiled=True)  15.2 us
    pallas_call x1, Pallas kernels, main_attention(): pl.pallas_call(main_kernel, grid_spec=pltpu.PrefetchScalarGridSpec(num_sc...  11.8 us
    unnamed x50, local copies, waits for them, and re-layouts  10.8 us
    ppermute x4, waiting for transfers between devices, move_x(): return lax.ppermute(a, 'span', span_route(dx=d))  9.1 us
    all_to_all x1, waiting for transfers between devices, per_device(): lax.all_to_all(jnp.broadcast_to(latents, (NY * NZ * NC, BLK, pv)), 'seq',...  8.94 us
  transfers between devices with their start and end apart: 30, of which 12 were waited for; matrix products, arithmetic and copies ran while one was open for 13% of the time, Pallas kernels for 8%

profile of v1, /device:TPU:10, one launch (start us, length us, event | category | flops | bytes accessed | tf_op | source)
XLA Modules:
  0.0 216.2 jit_solution(9818166272744997330)
XLA Ops:
  7.9 1.1 convert_reduce_fusion
  8.9 1.2 fusion.9
  10.1 1.0 constant_dynamic-slice_fusion
  11.2 1.7 constant_dynamic-update-slice_fusion.17
  12.9 5.9 %collective-permute-start = (bf16[32,3072]{1,0:T(8,128)(2,1)S(1)}, bf16[32,3072]{1,0:T(8,128)(2,1)S(1)}, u32[]{:S(2)}, u32[]{:S(2)}) collective-permute-start(bf16[32,3072]{1,0:T(8,128)(2,1)S(1)} %get-tuple-element.5), channel_id=1, source_target_pairs={{0,14},{1,15},{2,0},{3,1},{4,2},{5,3},{6,4},{7,5},{8,6},{9,7},{10,... | collective-permute-start | bytes 589832 | tf_op jit(solution)/shard_map/ppermute | solution.py:48
  19.2 1.2 select_bitcast_fusion
  20.4 0.6 collective-permute-start.24
  21.0 1.9 collective-permute-done
  22.9 3.7 %collective-permute-start.1 = (bf16[32,3072]{1,0:T(8,128)(2,1)S(1)}, bf16[32,3072]{1,0:T(8,128)(2,1)S(1)}, u32[]{:S(2)}, u32[]{:S(2)}) collective-permute-start(bf16[32,3072]{1,0:T(8,128)(2,1)S(1)} %collective-permute-done), channel_id=1, source_target_pairs={{0,14},{1,15},{2,0},{3,1},{4,2},{5,3},{6,4},{7,5},{8,6},{9,7},{10,... | collective-permute-start | bytes 589832 | tf_op jit(solution)/shard_map/ppermute | solution.py:48
  26.6 0.7 constant_dynamic-update-slice_fusion.16
  27.3 2.6 %collective-permute-done.1 = bf16[32,3072]{1,0:T(8,128)(2,1)S(1)} collective-permute-done((bf16[32,3072]{1,0:T(8,128)(2,1)S(1)}, bf16[32,3072]{1,0:T(8,128)(2,1)S(1)}, u32[]{:S(2)}, u32[]{:S(2)}) %collective-permute-start.1) | collective-permute-done | bytes 196640 | tf_op jit(solution)/shard_map/ppermute | solution.py:48
  29.9 3.7 %collective-permute-start.2 = (bf16[32,3072]{1,0:T(8,128)(2,1)S(1)}, bf16[32,3072]{1,0:T(8,128)(2,1)S(1)}, u32[]{:S(2)}, u32[]{:S(2)}) collective-permute-start(bf16[32,3072]{1,0:T(8,128)(2,1)S(1)} %collective-permute-done.1), channel_id=1, source_target_pairs={{0,14},{1,15},{2,0},{3,1},{4,2},{5,3},{6,4},{7,5},{8,6},{9,7},{10,... | collective-permute-start | bytes 589832 | tf_op jit(solution)/shard_map/ppermute | solution.py:48
  33.6 0.7 constant_dynamic-update-slice_fusion.15
  34.3 6.2 %collective-permute-done.5 = bf16[32,3072]{1,0:T(8,128)(2,1)S(1)} collective-permute-done((bf16[32,3072]{1,0:T(8,128)(2,1)S(1)}, bf16[32,3072]{1,0:T(8,128)(2,1)S(1)}, u32[]{:S(2)}, u32[]{:S(2)}) %collective-permute-start.5) | collective-permute-done | bytes 196640 | tf_op jit(solution)/shard_map/ppermute | solution.py:48
  41.0 0.7 constant_dynamic-update-slice_fusion.14
  41.7 5.1 %collective-permute-done.6 = bf16[16,3072]{1,0:T(8,128)(2,1)S(1)} collective-permute-done((bf16[16,3072]{1,0:T(8,128)(2,1)S(1)}, bf16[16,3072]{1,0:T(8,128)(2,1)S(1)}, u32[]{:S(2)}, u32[]{:S(2)}) %collective-permute-start.6) | collective-permute-done | bytes 98336 | tf_op jit(solution)/shard_map/ppermute | solution.py:48
  46.8 0.6 constant_dynamic-update-slice_fusion.13
  47.5 4.0 %collective-permute-done.7 = bf16[16,3072]{1,0:T(8,128)(2,1)S(1)} collective-permute-done((bf16[16,3072]{1,0:T(8,128)(2,1)S(1)}, bf16[16,3072]{1,0:T(8,128)(2,1)S(1)}, u32[]{:S(2)}, u32[]{:S(2)}) %collective-permute-start.7) | collective-permute-done | bytes 98336 | tf_op jit(solution)/shard_map/ppermute | solution.py:48
  51.5 1.6 collective-permute-start.10
  53.0 0.6 constant_dynamic-update-slice_fusion.12
  53.7 0.7 constant_dynamic-update-slice_fusion.11
  54.4 0.7 constant_dynamic-update-slice_fusion.10
  55.1 0.7 constant_dynamic-update-slice_fusion.9
  56.2 0.7 constant_dynamic-update-slice_fusion.8
  56.9 1.6 collective-permute-start.16
  58.5 1.4 collective-permute-start.11
  59.9 1.5 collective-permute-done.12
  61.5 0.7 constant_dynamic-update-slice_fusion.7
  62.1 0.7 constant_dynamic-update-slice_fusion.6
  62.8 5.5 %collective-permute-done.13 = bf16[32,3072]{1,0:T(8,128)(2,1)S(1)} collective-permute-done((bf16[32,3072]{1,0:T(8,128)(2,1)S(1)}, bf16[32,3072]{1,0:T(8,128)(2,1)S(1)}, u32[]{:S(2)}, u32[]{:S(2)}) %collective-permute-start.13) | collective-permute-done | bytes 196640 | tf_op jit(solution)/shard_map/ppermute | solution.py:48
  68.5 3.3 %collective-permute-start.15 = (bf16[16,3072]{1,0:T(8,128)(2,1)S(1)}, bf16[16,3072]{1,0:T(8,128)(2,1)S(1)}, u32[]{:S(2)}, u32[]{:S(2)}) collective-permute-start(bf16[16,3072]{1,0:T(8,128)(2,1)S(1)} %slice.195), channel_id=1, source_target_pairs={{0,14},{1,15},{2,0},{3,1},{4,2},{5,3},{6,4},{7,5},{8,6},{9,7},{10,... | collective-permute-start | bytes 294920 | tf_op jit(solution)/shard_map/ppermute | solution.py:48
  71.8 1.3 pad_maximum_fusion
  73.1 1.2 collective-permute-done.14
  74.4 0.5 collective-permute-start.25
  74.9 3.6 %convolution_convert_fusion = bf16[512,384]{1,0:T(8,128)(2,1)S(1)} fusion(bf16[512,3072]{1,0:T(8,128)(2,1)S(1)} %constant_dynamic-update-slice_fusion, bf16[3072,384]{1,0:T(8,128)(2,1)} %collective-permute-done.17), kind=kOutput, calls=%fused_computation.6 | convolution fusion | flops 1208156160 | bytes 5898240 | tf_op jit(solution)/shard_map/dot_general | solution.py:286
  78.7 1.8 convolution_convert_fusion.1
  80.5 1.6 collective-permute-start.20
  82.1 0.5 collective-permute-start.21
  82.7 0.7 pad_add_fusion.s_ref
  83.3 2.5 %collective-permute-start.19 = (bf16[1024,128]{1,0:T(8,128)(2,1)S(1)}, bf16[1024,128]{1,0:T(8,128)(2,1)S(1)}, u32[]{:S(2)}, u32[]{:S(2)}) collective-permute-start(bf16[1024,128]{1,0:T(8,128)(2,1)S(1)} %pad_maximum_fusion.3.qa_ref.q_ref), channel_id=1, source_target_pairs={{0,32},{32,0},{64,96},{96,64},{128,160},{160,128},{192,224},{224,1... | collective-permute-start | bytes 786440 | tf_op jit(solution)/shard_map/ppermute | solution.py:64
  85.9 9.1 %collective-permute-done.20.k1 = bf16[1024,256]{1,0:T(8,128)(2,1)S(1)} collective-permute-done((bf16[1024,256]{1,0:T(8,128)(2,1)S(1)}, bf16[1024,256]{1,0:T(8,128)(2,1)S(1)}, u32[]{:S(2)}, u32[]{:S(2)}) %collective-permute-start.20) | collective-permute-done | bytes 524320 | tf_op jit(solution)/shard_map/ppermute | solution.py:60
  95.0 1.6 collective-permute-start.22
  96.6 0.7 slice.197
  97.3 0.5 collective-permute-start.23
  97.8 0.7 fusion.25
  107.3 2.9 %fusion.1 = f32[128,64]{0,1:T(8,128)} fusion(bf16[3072,64]{0,1:T(8,128)(2,1)S(1)} %copy-done, bf16[128,3072]{1,0:T(8,128)(2,1)} %copy-done.1, f32[3072]{0:T(1024)S(1)} %bitcast.65), kind=kOutput, calls=%fused_computation.3 | convolution fusion | flops 302776320 | bytes 1224704 | tf_op jit(solution)/shard_map/dot_general | solution.py:301
  110.1 2.7 %self_attention.1 = bf16[1024,128]{1,0:T(8,128)(2,1)S(1)} custom-call(bf16[1024,128]{1,0:T(8,128)(2,1)S(1)} %pad_maximum_fusion.3.qa_ref.q_ref, bf16[1024,256]{1,0:T(8,128)(2,1)S(1)} %pad_maximum_fusion.2.k0.kv_ref), custom_call_target="tpu_custom_call" | custom-call | tf_op jit(solution)/shard_map/self_attention/pallas_call | solution.py:109
  112.8 11.8 %main_attention.1 = bf16[8,272,128]{2,1,0:T(8,128)(2,1)} custom-call(s32[9]{0:T(128)S(1)} %concatenate.21.s_ref, bf16[1024,128]{1,0:T(8,128)(2,1)S(1)} %pad_maximum_fusion.3.qa_ref.q_ref, bf16[1024,128]{1,0:T(8,128)(2,1)S(1)} %collective-permute-done.19.qb_ref, bf16[1024,256]{1,0:T(8,128)(2,1)S(1)} %pad_maximum_fusion.2.k0.kv_ref, ...), custom_call_target="tpu_custom_call" | custom-call | tf_op jit(solution)/shard_map/main_attention/pallas_call | solution.py:171
  124.7 17.8 %all-to-all-start = ((bf16[8,272,128]{2,1,0:T(8,128)(2,1)}), bf16[8,272,128]{2,1,0:T(8,128)(2,1)S(1)}, u32[]{:S(2)}, u32[]{:S(2)}) async-start(bf16[8,272,128]{2,1,0:T(8,128)(2,1)} %main_attention.1), calls=%async_computation | async-start | bytes 1114112 | tf_op jit(solution)/shard_map/all_to_all | solution.py:343
  143.2 8.5 %all-to-all-done.in_ref = bf16[8,272,128]{2,1,0:T(8,128)(2,1)S(1)} async-done(((bf16[8,272,128]{2,1,0:T(8,128)(2,1)}), bf16[8,272,128]{2,1,0:T(8,128)(2,1)S(1)}, u32[]{:S(2)}, u32[]{:S(2)}) %all-to-all-start) | async-done | bytes 557088 | tf_op jit(solution)/shard_map/all_to_all | solution.py:343
  151.7 0.8 copy-done.6
  152.5 2.8 %join_heads.1 = bf16[256,512]{1,0:T(8,128)(2,1)} custom-call(s32[2]{0:T(128)} %pad_add_fusion.s_ref, bf16[8,272,128]{2,1,0:T(8,128)(2,1)} %copy-done.6), custom_call_target="tpu_custom_call" | custom-call | tf_op jit(solution)/shard_map/join_heads/pallas_call | solution.py:222
  155.3 2.1 fusion.18
  157.4 1.8 fusion
  159.6 15.2 %all_to_all.20 = bf16[32,2,1024]{2,1,0:T(2,128)(2,1)S(1)} all-to-all(bf16[32,2,1024]{2,1,0:T(2,128)(2,1)S(1)} %reshape.111), channel_id=1, replica_groups=mesh['span'=8,'seq'=32] {'seq'}, dimensions={0} | all-to-all | bytes 262144 | tf_op jit(solution)/shard_map/all_to_all | solution.py:312
  175.5 0.7 reshape.113
  176.2 7.3 %all-to-all-start.2 = ((bf16[8,2,1024]{2,1,0:T(2,128)(2,1)}), bf16[8,2,1024]{2,1,0:T(2,128)(2,1)S(1)}, u32[]{:S(2)}, u32[]{:S(2)}) async-start(bf16[8,2,1024]{2,1,0:T(2,128)(2,1)} %reshape.113), calls=%async_computation.3 | async-start | bytes 65536 | tf_op jit(solution)/shard_map/all_to_all | solution.py:319
  183.5 0.6 fusion.21
  186.1 3.7 %all-to-all-done.2 = bf16[8,2,1024]{2,1,0:T(2,128)(2,1)S(1)} async-done(((bf16[8,2,1024]{2,1,0:T(2,128)(2,1)}), bf16[8,2,1024]{2,1,0:T(2,128)(2,1)S(1)}, u32[]{:S(2)}, u32[]{:S(2)}) %all-to-all-start.2) | async-done | bytes 32800 | tf_op jit(solution)/shard_map/all_to_all | solution.py:319
  190.0 0.8 reshape.115
  190.8 5.2 %all-to-all-start.3 = ((bf16[32,2,1024]{2,1,0:T(2,128)(2,1)}), bf16[32,2,1024]{2,1,0:T(2,128)(2,1)S(1)}, u32[]{:S(2)}, u32[]{:S(2)}) async-start(bf16[32,2,1024]{2,1,0:T(2,128)(2,1)} %reshape.115), calls=%async_computation.4 | async-start | bytes 262144 | tf_op jit(solution)/shard_map/all_to_all | solution.py:323
  196.1 8.9 %all-to-all-done.3 = bf16[32,2,1024]{2,1,0:T(2,128)(2,1)S(1)} async-done(((bf16[32,2,1024]{2,1,0:T(2,128)(2,1)}), bf16[32,2,1024]{2,1,0:T(2,128)(2,1)S(1)}, u32[]{:S(2)}, u32[]{:S(2)}) %all-to-all-start.3) | async-done | bytes 131104 | tf_op jit(solution)/shard_map/all_to_all | solution.py:323
  206.9 0.8 fusion.4
  207.7 1.7 fusion.16
  (106 shorter events, 5.5 us)
Async XLA Ops:
  7.2 100.1 %copy-start = (bf16[3072,64]{0,1:T(8,128)(2,1)S(1)}, bf16[3072,64]{0,1:T(8,128)(2,1)}, u32[]{:S(2)}) copy-start(bf16[3072,64]{0,1:T(8,128)(2,1)} %param.14) | copy-start | bytes 1179652
  12.9 10.0 %collective-permute-start = (bf16[32,3072]{1,0:T(8,128)(2,1)S(1)}, bf16[32,3072]{1,0:T(8,128)(2,1)S(1)}, u32[]{:S(2)}, u32[]{:S(2)}) collective-permute-start(bf16[32,3072]{1,0:T(8,128)(2,1)S(1)} %get-tuple-element.5), channel_id=1, source_target_pairs={{0,14},{1,15},{2,0},{3,1},{4,2},{5,3},{6,4},{7,5},{8,6},{9,7},{10,... | collective-permute-start | bytes 589832 | tf_op jit(solution)/shard_map/ppermute | solution.py:48
  18.8 7.9 %collective-permute-start.3 = (bf16[32,3072]{1,0:T(8,128)(2,1)S(1)}, bf16[32,3072]{1,0:T(8,128)(2,1)S(1)}, u32[]{:S(2)}, u32[]{:S(2)}) collective-permute-start(bf16[32,3072]{1,0:T(8,128)(2,1)S(1)} %get-tuple-element.5), channel_id=1, source_target_pairs={{0,2},{1,3},{2,4},{3,5},{4,6},{5,7},{6,8},{7,9},{8,10},{9,11},{10,... | collective-permute-start | bytes 589832 | tf_op jit(solution)/shard_map/ppermute | solution.py:48
  18.8 37.0 %collective-permute-start.8 = (bf16[32,3072]{1,0:T(8,128)(2,1)S(1)}, bf16[32,3072]{1,0:T(8,128)(2,1)S(1)}, u32[]{:S(2)}, u32[]{:S(2)}) collective-permute-start(bf16[32,3072]{1,0:T(8,128)(2,1)S(1)} %get-tuple-element.5), channel_id=1, source_target_pairs={{0,16},{1,17},{2,18},{3,19},{4,20},{5,21},{6,22},{7,23},{8,24},{9,... | collective-permute-start | bytes 589832 | tf_op jit(solution)/shard_map/ppermute | solution.py:52
  19.2 55.7 %collective-permute-start.17 = (bf16[3072,384]{1,0:T(8,128)(2,1)}, bf16[3072,384]{1,0:T(8,128)(2,1)}, u32[]{:S(2)}, u32[]{:S(2)}) collective-permute-start(bf16[3072,384]{1,0:T(8,128)(2,1)} %bitcast.70), channel_id=1, source_target_pairs={{0,1},{1,0},{2,3},{3,2},{4,5},{5,4},{6,7},{7,6},{8,9},{9,8},{10,11... | collective-permute-start | bytes 7077896 | tf_op jit(solution)/shard_map/ppermute | solution.py:56
  20.4 52.7 %copy-start.1 = (bf16[128,3072]{1,0:T(8,128)(2,1)}, bf16[128,3072]{1,0:T(8,128)(2,1)S(1)}, u32[]{:S(2)}) copy-start(bf16[128,3072]{1,0:T(8,128)(2,1)S(1)} %select_bitcast_fusion) | copy-start | bytes 2359300
  20.4 51.3 %collective-permute-start.24 = (bf16[128,3072]{1,0:T(8,128)(2,1)S(1)}, bf16[128,3072]{1,0:T(8,128)(2,1)S(1)}, u32[]{:S(2)}, u32[]{:S(2)}) collective-permute-start(bf16[128,3072]{1,0:T(8,128)(2,1)S(1)} %select_bitcast_fusion), channel_id=1, source_target_pairs={{0,1},{1,0},{2,3},{3,2},{4,5},{5,4},{6,7},{7,6},{8,9},{9,8},{10,11... | collective-permute-start | bytes 2359304 | tf_op jit(solution)/shard_map/ppermute | solution.py:56
  22.9 7.0 %collective-permute-start.1 = (bf16[32,3072]{1,0:T(8,128)(2,1)S(1)}, bf16[32,3072]{1,0:T(8,128)(2,1)S(1)}, u32[]{:S(2)}, u32[]{:S(2)}) collective-permute-start(bf16[32,3072]{1,0:T(8,128)(2,1)S(1)} %collective-permute-done), channel_id=1, source_target_pairs={{0,14},{1,15},{2,0},{3,1},{4,2},{5,3},{6,4},{7,5},{8,6},{9,7},{10,... | collective-permute-start | bytes 589832 | tf_op jit(solution)/shard_map/ppermute | solution.py:48
  26.6 7.0 %collective-permute-start.4 = (bf16[32,3072]{1,0:T(8,128)(2,1)S(1)}, bf16[32,3072]{1,0:T(8,128)(2,1)S(1)}, u32[]{:S(2)}, u32[]{:S(2)}) collective-permute-start(bf16[32,3072]{1,0:T(8,128)(2,1)S(1)} %collective-permute-done.3), channel_id=1, source_target_pairs={{0,2},{1,3},{2,4},{3,5},{4,6},{5,7},{6,8},{7,9},{8,10},{9,11},{10,... | collective-permute-start | bytes 589832 | tf_op jit(solution)/shard_map/ppermute | solution.py:48
  29.9 11.0 %collective-permute-start.2 = (bf16[32,3072]{1,0:T(8,128)(2,1)S(1)}, bf16[32,3072]{1,0:T(8,128)(2,1)S(1)}, u32[]{:S(2)}, u32[]{:S(2)}) collective-permute-start(bf16[32,3072]{1,0:T(8,128)(2,1)S(1)} %collective-permute-done.1), channel_id=1, source_target_pairs={{0,14},{1,15},{2,0},{3,1},{4,2},{5,3},{6,4},{7,5},{8,6},{9,7},{10,... | collective-permute-start | bytes 589832 | tf_op jit(solution)/shard_map/ppermute | solution.py:48
  33.6 6.9 %collective-permute-start.5 = (bf16[32,3072]{1,0:T(8,128)(2,1)S(1)}, bf16[32,3072]{1,0:T(8,128)(2,1)S(1)}, u32[]{:S(2)}, u32[]{:S(2)}) collective-permute-start(bf16[32,3072]{1,0:T(8,128)(2,1)S(1)} %collective-permute-done.4), channel_id=1, source_target_pairs={{0,2},{1,3},{2,4},{3,5},{4,6},{5,7},{6,8},{7,9},{8,10},{9,11},{10,... | collective-permute-start | bytes 589832 | tf_op jit(solution)/shard_map/ppermute | solution.py:48
  40.5 16.4 %collective-permute-start.9 = (bf16[32,3072]{1,0:T(8,128)(2,1)S(1)}, bf16[32,3072]{1,0:T(8,128)(2,1)S(1)}, u32[]{:S(2)}, u32[]{:S(2)}) collective-permute-start(bf16[32,3072]{1,0:T(8,128)(2,1)S(1)} %collective-permute-done), channel_id=1, source_target_pairs={{0,16},{1,17},{2,18},{3,19},{4,20},{5,21},{6,22},{7,23},{8,24},{9,... | collective-permute-start | bytes 589832 | tf_op jit(solution)/shard_map/ppermute | solution.py:52
  40.9 5.9 %collective-permute-start.6 = (bf16[16,3072]{1,0:T(8,128)(2,1)S(1)}, bf16[16,3072]{1,0:T(8,128)(2,1)S(1)}, u32[]{:S(2)}, u32[]{:S(2)}) collective-permute-start(bf16[16,3072]{1,0:T(8,128)(2,1)S(1)} %slice.192), channel_id=1, source_target_pairs={{0,2},{1,3},{2,4},{3,5},{4,6},{5,7},{6,8},{7,9},{8,10},{9,11},{10,... | collective-permute-start | bytes 294920 | tf_op jit(solution)/shard_map/ppermute | solution.py:48
  46.8 4.6 %collective-permute-start.7 = (bf16[16,3072]{1,0:T(8,128)(2,1)S(1)}, bf16[16,3072]{1,0:T(8,128)(2,1)S(1)}, u32[]{:S(2)}, u32[]{:S(2)}) collective-permute-start(bf16[16,3072]{1,0:T(8,128)(2,1)S(1)} %slice.193), channel_id=1, source_target_pairs={{0,14},{1,15},{2,0},{3,1},{4,2},{5,3},{6,4},{7,5},{8,6},{9,7},{10,... | collective-permute-start | bytes 294920 | tf_op jit(solution)/shard_map/ppermute | solution.py:48
  51.5 7.0 %collective-permute-start.10 = (bf16[32,3072]{1,0:T(8,128)(2,1)S(1)}, bf16[32,3072]{1,0:T(8,128)(2,1)S(1)}, u32[]{:S(2)}, u32[]{:S(2)}) collective-permute-start(bf16[32,3072]{1,0:T(8,128)(2,1)S(1)} %collective-permute-done.1), channel_id=1, source_target_pairs={{0,16},{1,17},{2,18},{3,19},{4,20},{5,21},{6,22},{7,23},{8,24},{9,... | collective-permute-start | bytes 589832 | tf_op jit(solution)/shard_map/ppermute | solution.py:52
  55.8 5.7 %collective-permute-start.12 = (bf16[32,3072]{1,0:T(8,128)(2,1)S(1)}, bf16[32,3072]{1,0:T(8,128)(2,1)S(1)}, u32[]{:S(2)}, u32[]{:S(2)}) collective-permute-start(bf16[32,3072]{1,0:T(8,128)(2,1)S(1)} %collective-permute-done.4), channel_id=1, source_target_pairs={{0,16},{1,17},{2,18},{3,19},{4,20},{5,21},{6,22},{7,23},{8,24},{9,... | collective-permute-start | bytes 589832 | tf_op jit(solution)/shard_map/ppermute | solution.py:52
  56.9 17.4 %collective-permute-start.16 = (bf16[32,3072]{1,0:T(8,128)(2,1)S(1)}, bf16[32,3072]{1,0:T(8,128)(2,1)S(1)}, u32[]{:S(2)}, u32[]{:S(2)}) collective-permute-start(bf16[32,3072]{1,0:T(8,128)(2,1)S(1)} %collective-permute-done.3), channel_id=1, source_target_pairs={{0,16},{1,17},{2,18},{3,19},{4,20},{5,21},{6,22},{7,23},{8,24},{9,... | collective-permute-start | bytes 589832 | tf_op jit(solution)/shard_map/ppermute | solution.py:52
  58.5 9.9 %collective-permute-start.11 = (bf16[32,3072]{1,0:T(8,128)(2,1)S(1)}, bf16[32,3072]{1,0:T(8,128)(2,1)S(1)}, u32[]{:S(2)}, u32[]{:S(2)}) collective-permute-start(bf16[32,3072]{1,0:T(8,128)(2,1)S(1)} %collective-permute-done.10), channel_id=1, source_target_pairs={{0,14},{1,15},{2,0},{3,1},{4,2},{5,3},{6,4},{7,5},{8,6},{9,7},{10,... | collective-permute-start | bytes 589832 | tf_op jit(solution)/shard_map/ppermute | solution.py:48
  61.5 6.9 %collective-permute-start.13 = (bf16[32,3072]{1,0:T(8,128)(2,1)S(1)}, bf16[32,3072]{1,0:T(8,128)(2,1)S(1)}, u32[]{:S(2)}, u32[]{:S(2)}) collective-permute-start(bf16[32,3072]{1,0:T(8,128)(2,1)S(1)} %collective-permute-done.12), channel_id=1, source_target_pairs={{0,2},{1,3},{2,4},{3,5},{4,6},{5,7},{6,8},{7,9},{8,10},{9,11},{10,... | collective-permute-start | bytes 589832 | tf_op jit(solution)/shard_map/ppermute | solution.py:48
  62.8 10.2 %copy-start.12 = (bf16[512,3072]{1,0:T(8,128)(2,1)S(1)}, bf16[512,3072]{1,0:T(8,128)(2,1)}, u32[]{:S(2)}) copy-start(bf16[512,3072]{1,0:T(8,128)(2,1)} %constant_dynamic-update-slice_fusion.6) | copy-start | bytes 9437188
  68.3 5.9 %collective-permute-start.14 = (bf16[16,3072]{1,0:T(8,128)(2,1)S(1)}, bf16[16,3072]{1,0:T(8,128)(2,1)S(1)}, u32[]{:S(2)}, u32[]{:S(2)}) collective-permute-start(bf16[16,3072]{1,0:T(8,128)(2,1)S(1)} %slice.194), channel_id=1, source_target_pairs={{0,2},{1,3},{2,4},{3,5},{4,6},{5,7},{6,8},{7,9},{8,10},{9,11},{10,... | collective-permute-start | bytes 294920 | tf_op jit(solution)/shard_map/ppermute | solution.py:48
  68.5 5.8 %collective-permute-start.15 = (bf16[16,3072]{1,0:T(8,128)(2,1)S(1)}, bf16[16,3072]{1,0:T(8,128)(2,1)S(1)}, u32[]{:S(2)}, u32[]{:S(2)}) collective-permute-start(bf16[16,3072]{1,0:T(8,128)(2,1)S(1)} %slice.195), channel_id=1, source_target_pairs={{0,14},{1,15},{2,0},{3,1},{4,2},{5,3},{6,4},{7,5},{8,6},{9,7},{10,... | collective-permute-start | bytes 294920 | tf_op jit(solution)/shard_map/ppermute | solution.py:48
  71.8 6.8 %copy-start.4 = (bf16[128,3072]{1,0:T(8,128)(2,1)}, bf16[128,3072]{1,0:T(8,128)(2,1)S(1)}, u32[]{:S(2)}) copy-start(bf16[128,3072]{1,0:T(8,128)(2,1)S(1)} %collective-permute-done.24) | copy-start | bytes 2359300
  74.4 4.3 %copy-start.13 = (bf16[1,3072,384]{2,1,0:T(8,128)(2,1)S(1)}, bf16[1,3072,384]{2,1,0:T(8,128)(2,1)}, u32[]{:S(2)}) copy-start(bf16[1,3072,384]{2,1,0:T(8,128)(2,1)} %param.12) | copy-start | bytes 7077892
  74.4 80.9 %collective-permute-start.25 = (bf16[256,3072]{1,0:T(8,128)(2,1)}, bf16[256,3072]{1,0:T(8,128)(2,1)}, u32[]{:S(2)}, u32[]{:S(2)}) collective-permute-start(bf16[256,3072]{1,0:T(8,128)(2,1)} %pad_maximum_fusion), channel_id=1, source_target_pairs={{0,16},{1,17},{2,18},{3,19},{4,20},{5,21},{6,22},{7,23},{8,24},{9,... | collective-permute-start | bytes 4718600 | tf_op jit(solution)/shard_map/ppermute | solution.py:52
  78.6 1.9 collective-permute-start.18
  80.5 17.3 %copy-start.10 = (s32[8]{0:T(128)S(1)}, s32[8]{0:T(128)}, u32[]{:S(2)}) copy-start(s32[8]{0:T(128)} %param.10) | copy-start | bytes 100
  80.5 14.4 %collective-permute-start.20 = (bf16[1024,256]{1,0:T(8,128)(2,1)S(1)}, bf16[1024,256]{1,0:T(8,128)(2,1)S(1)}, u32[]{:S(2)}, u32[]{:S(2)}) collective-permute-start(bf16[1024,256]{1,0:T(8,128)(2,1)S(1)} %pad_maximum_fusion.2.k0.kv_ref), channel_id=1, source_target_pairs={{0,64},{32,96},{64,128},{96,160},{128,192},{160,224},{192,0},{224,... | collective-permute-start | bytes 1572872 | tf_op jit(solution)/shard_map/ppermute | solution.py:60
  82.1 14.4 %collective-permute-start.21 = (bf16[1024,256]{1,0:T(8,128)(2,1)S(1)}, bf16[1024,256]{1,0:T(8,128)(2,1)S(1)}, u32[]{:S(2)}, u32[]{:S(2)}) collective-permute-start(bf16[1024,256]{1,0:T(8,128)(2,1)S(1)} %pad_maximum_fusion.2.k0.kv_ref), channel_id=1, source_target_pairs={{0,192},{32,224},{64,0},{96,32},{128,64},{160,96},{192,128},{224,1... | collective-permute-start | bytes 1572872 | tf_op jit(solution)/shard_map/ppermute | solution.py:60
  83.3 29.5 %collective-permute-start.19 = (bf16[1024,128]{1,0:T(8,128)(2,1)S(1)}, bf16[1024,128]{1,0:T(8,128)(2,1)S(1)}, u32[]{:S(2)}, u32[]{:S(2)}) collective-permute-start(bf16[1024,128]{1,0:T(8,128)(2,1)S(1)} %pad_maximum_fusion.3.qa_ref.q_ref), channel_id=1, source_target_pairs={{0,32},{32,0},{64,96},{96,64},{128,160},{160,128},{192,224},{224,1... | collective-permute-start | bytes 786440 | tf_op jit(solution)/shard_map/ppermute | solution.py:64
  95.0 17.8 %collective-permute-start.22 = (bf16[512,256]{1,0:T(8,128)(2,1)S(1)}, bf16[512,256]{1,0:T(8,128)(2,1)S(1)}, u32[]{:S(2)}, u32[]{:S(2)}) collective-permute-start(bf16[512,256]{1,0:T(8,128)(2,1)S(1)} %slice.196), channel_id=1, source_target_pairs={{0,64},{32,96},{64,128},{96,160},{128,192},{160,224},{192,0},{224,... | collective-permute-start | bytes 786440 | tf_op jit(solution)/shard_map/ppermute | solution.py:60
  97.3 15.6 %collective-permute-start.23 = (bf16[512,256]{1,0:T(8,128)(2,1)}, bf16[512,256]{1,0:T(8,128)(2,1)S(1)}, u32[]{:S(2)}, u32[]{:S(2)}) collective-permute-start(bf16[512,256]{1,0:T(8,128)(2,1)} %slice.197), channel_id=1, source_target_pairs={{0,192},{32,224},{64,0},{96,32},{128,64},{160,96},{192,128},{224,1... | collective-permute-start | bytes 786440 | tf_op jit(solution)/shard_map/ppermute | solution.py:60
  112.8 29.6 %copy-start.8 = (f32[128,64]{0,1:T(8,128)S(1)}, f32[128,64]{0,1:T(8,128)}, u32[]{:S(2)}) copy-start(f32[128,64]{0,1:T(8,128)} %fusion.1) | copy-start | bytes 98308
  124.7 27.0 %all-to-all-start = ((bf16[8,272,128]{2,1,0:T(8,128)(2,1)}), bf16[8,272,128]{2,1,0:T(8,128)(2,1)S(1)}, u32[]{:S(2)}, u32[]{:S(2)}) async-start(bf16[8,272,128]{2,1,0:T(8,128)(2,1)} %main_attention.1), calls=%async_computation | async-start | bytes 1114112 | tf_op jit(solution)/shard_map/all_to_all | solution.py:343
  142.5 65.2 %reduce-scatter.2.cloned.1.call-start = ((), (), s32[]{:S(2)}) async-start(), calls=%async_computation.5 | async-start | bytes 1769472 | tf_op jit(solution)/shard_map/reduce_scatter | solution.py:351
  143.1 14.3 %copy-start.2 = (bf16[128,3072]{1,0:T(8,128)(2,1)S(1)}, bf16[128,3072]{1,0:T(8,128)(2,1)}, u32[]{:S(2)}) copy-start(bf16[128,3072]{1,0:T(8,128)(2,1)} %copy-done.1) | copy-start | bytes 2359300
  143.1 14.3 %copy-start.5 = (bf16[128,3072]{1,0:T(8,128)(2,1)S(1)}, bf16[128,3072]{1,0:T(8,128)(2,1)}, u32[]{:S(2)}) copy-start(bf16[128,3072]{1,0:T(8,128)(2,1)} %copy-done.4) | copy-start | bytes 2359300
  151.7 0.8 copy-start.6
  155.3 2.1 copy-start.7
  159.2 16.0 %copy-start.3 = (bf16[1,32,3072]{2,1,0:T(8,128)(2,1)S(1)}, bf16[1,32,3072]{2,1,0:T(8,128)(2,1)}, u32[]{:S(2)}) copy-start(bf16[1,32,3072]{2,1,0:T(8,128)(2,1)} %param.8) | copy-start | bytes 589828
  159.2 24.3 %copy-start.11 = (s32[8]{0:T(128)S(1)}, s32[8]{0:T(128)}, u32[]{:S(2)}) copy-start(s32[8]{0:T(128)} %param.10) | copy-start | bytes 100
  176.2 13.6 %all-to-all-start.2 = ((bf16[8,2,1024]{2,1,0:T(2,128)(2,1)}), bf16[8,2,1024]{2,1,0:T(2,128)(2,1)S(1)}, u32[]{:S(2)}, u32[]{:S(2)}) async-start(bf16[8,2,1024]{2,1,0:T(2,128)(2,1)} %reshape.113), calls=%async_computation.3 | async-start | bytes 65536 | tf_op jit(solution)/shard_map/all_to_all | solution.py:319
  190.8 16.1 %copy-start.9 = (bf16[3,3,3,16,64]{4,3,2,1,0:T(8,128)(2,1)S(1)}, bf16[3,3,3,16,64]{4,3,2,1,0:T(8,128)(2,1)}, u32[]{:S(2)}) copy-start(bf16[3,3,3,16,64]{4,3,2,1,0:T(8,128)(2,1)} %param.15) | copy-start | bytes 165892
  190.8 14.3 %all-to-all-start.3 = ((bf16[32,2,1024]{2,1,0:T(2,128)(2,1)}), bf16[32,2,1024]{2,1,0:T(2,128)(2,1)S(1)}, u32[]{:S(2)}, u32[]{:S(2)}) async-start(bf16[32,2,1024]{2,1,0:T(2,128)(2,1)} %reshape.115), calls=%async_computation.4 | async-start | bytes 262144 | tf_op jit(solution)/shard_map/all_to_all | solution.py:323
Sparse Core Ops, SparseCore 0:
  159.4 38.5 reduce-scatter.1

commit v2 on v1

v2 whole, which is shorter than its diff:
```python
import functools
import math

import jax
import jax.numpy as jnp
from jax import lax
from jax.experimental import pallas as pl
from jax.experimental.pallas import tpu as pltpu
from jax.sharding import PartitionSpec as P

HEADS = 24
FR = 4
P_SIZE = 2
C = 16
HD = 128

EPSILON = 1e-06
NEG_LARGE = 1e30

NX, NH, NY, NZ, NC = 4, 2, 2, 8, 2
BLK = 32
QUARTER = NZ * BLK
TAIL = 16


def seq_at(y, z, c):
    return ((y % NY) * NZ + z % NZ) * NC + c % NC


def span_at(x, h):
    return (x % NX) * NH + h % NH


def seq_route(dy=0, dz=0, dc=0):
    return [
        (seq_at(y, z, c), seq_at(y + dy, z + dz, c + dc))
        for y in range(NY)
        for z in range(NZ)
        for c in range(NC)
    ]


def span_route(dx=0, dh=0):
    return [(span_at(x, h), span_at(x + dx, h + dh)) for x in range(NX) for h in range(NH)]


def move_z(a, d):
    return lax.ppermute(a, "seq", seq_route(dz=d))


def move_y(a):
    return lax.ppermute(a, "seq", seq_route(dy=1))


def move_core(a):
    return lax.ppermute(a, "seq", seq_route(dc=1))


def move_x(a, d):
    return lax.ppermute(a, "span", span_route(dx=d))


def move_hi(a):
    return lax.ppermute(a, "span", span_route(dh=1))


def gather_class(b):
    up1, dn1, y0 = move_z(b, 1), move_z(b, -1), move_y(b)
    up2, dn2 = move_z(up1, 1), move_z(dn1, -1)
    yu1, yd1 = move_y(up1), move_y(dn1)
    up3, dn3 = move_z(up2, 1), move_z(dn2, -1)
    yu2, yd2 = move_y(up2), move_y(dn2)
    far = move_z(up3, 1)
    yu3, yd3 = move_z(yu2, 1), move_z(yd2, -1)
    yfar = move_y(far)
    return (b, dn1, dn2, dn3, far, up3, up2, up1), (y0, yd1, yd2, yd3, yfar, yu3, yu2, yu1)


VMEM_LIMIT = 40 * 2**20
EXP_SCALE = math.log2(math.e) / math.sqrt(HD)


def norm_kernel(level_ref, hidden_ref, mod_ref, out_ref, gate_ref):
    values = hidden_ref[...].astype(jnp.float32)
    center = values - jnp.mean(values, axis=-1, keepdims=True)
    spread = jnp.mean(center * center, axis=-1, keepdims=True)
    scaled = center * lax.rsqrt(spread + EPSILON)
    out_ref[...] = (scaled * (1.0 + mod_ref[0, 1:2, :]) + mod_ref[0, 0:1, :]).astype(jnp.bfloat16)
    gate_ref[...] = mod_ref[0, 2:3, :]


def normalize(levels, rows, modulation):
    width = rows.shape[1]
    return pl.pallas_call(
        norm_kernel,
        grid_spec=pltpu.PrefetchScalarGridSpec(
            num_scalar_prefetch=1,
            grid=(1,),
            in_specs=[
                pl.BlockSpec(rows.shape, lambda i, s: (0, 0)),
                pl.BlockSpec((1, 3, width), lambda i, s: (s[0], 0, 0)),
            ],
            out_specs=[
                pl.BlockSpec(rows.shape, lambda i, s: (0, 0)),
                pl.BlockSpec((1, width), lambda i, s: (0, 0)),
            ],
        ),
        out_shape=[
            jax.ShapeDtypeStruct(rows.shape, jnp.bfloat16),
            jax.ShapeDtypeStruct((1, width), jnp.float32),
        ],
        name="normalize",
    )(levels, rows, modulation)


def project_kernel(*refs):
    blocks, (own_ref, oth_ref, mine_ref, theirs_ref, rows) = refs[:NZ], refs[NZ:]
    for i, block in enumerate(blocks):
        rows[i * BLK : i * BLK + BLK, :] = block[...]
    for w_ref, o_ref in ((oth_ref, theirs_ref), (own_ref, mine_ref)):
        out = jnp.dot(rows[...], w_ref[...], preferred_element_type=jnp.float32)
        o_ref[:, :HD] = (out[:, :HD] * EXP_SCALE).astype(jnp.bfloat16)
        o_ref[:, HD:] = out[:, HD:].astype(jnp.bfloat16)


def project(blocks, w_own, w_oth):
    width, cols = w_own.shape
    rows = len(blocks) * BLK
    vmem = pl.BlockSpec(memory_space=pltpu.VMEM)
    return pl.pallas_call(
        project_kernel,
        in_specs=[vmem] * (len(blocks) + 2),
        out_specs=[vmem, vmem],
        out_shape=[jax.ShapeDtypeStruct((rows, cols), jnp.bfloat16)] * 2,
        scratch_shapes=[pltpu.VMEM((rows, width), jnp.bfloat16)],
        compiler_params=pltpu.CompilerParams(vmem_limit_bytes=VMEM_LIMIT),
        cost_estimate=pl.CostEstimate(
            flops=4 * rows * width * cols,
            bytes_accessed=4 * width * cols + 2 * rows * width,
            transcendentals=0,
        ),
        name="project",
    )(*blocks, w_own, w_oth)


def dot_t(a, b):
    return lax.dot_general(a, b, (((1,), (1,)), ((), ())), preferred_element_type=jnp.float32)


TILE = 128


def self_kernel(s_ref, q_ref, kv_ref, hi_ref, lo_ref, o_ref, values):
    y, z, core = s_ref[1], s_ref[2], s_ref[3]
    values[:, :HD] = kv_ref[:, HD:]
    values[:, HD:] = jnp.ones((values.shape[0], HD), jnp.bfloat16)
    for t in range(q_ref.shape[0] // TILE):
        s = dot_t(q_ref[t * TILE : t * TILE + TILE, :], kv_ref[:, :HD])
        p = jnp.exp2(s - jnp.max(s, axis=1, keepdims=True)).astype(jnp.bfloat16)
        acc = jnp.dot(p, values[...], preferred_element_type=jnp.float32)
        att = (acc[:, :HD] / acc[:, HD:]).astype(jnp.bfloat16)
        part = jnp.dot(att, hi_ref[...], preferred_element_type=jnp.float32) + jnp.dot(
            att, lo_ref[...], preferred_element_type=jnp.float32
        )
        part = part.astype(jnp.bfloat16)
        for j in range(TILE // BLK):
            i = t * (TILE // BLK) + j
            d, quarter = i % NZ, i // NZ
            at = ((y ^ (quarter // 2)) * NZ + (z + d) % NZ) * NC + (core ^ (quarter % 2))
            o_ref[at] = part[j * BLK : j * BLK + BLK]


def self_attention(place, q, kv, hi, lo):
    pv = hi.shape[1]
    rows = q.shape[0]
    return pl.pallas_call(
        self_kernel,
        grid_spec=pltpu.PrefetchScalarGridSpec(
            num_scalar_prefetch=1,
            grid=(1,),
            in_specs=[pl.BlockSpec(a.shape, lambda i, s: (0, 0)) for a in (q, kv, hi, lo)],
            out_specs=pl.BlockSpec((rows // BLK, BLK, pv), lambda i, s: (0, 0, 0)),
            scratch_shapes=[pltpu.VMEM((rows, 2 * HD), jnp.bfloat16)],
        ),
        out_shape=jax.ShapeDtypeStruct((rows // BLK, BLK, pv), jnp.bfloat16),
        compiler_params=pltpu.CompilerParams(vmem_limit_bytes=VMEM_LIMIT),
        cost_estimate=pl.CostEstimate(
            flops=6 * rows * rows * HD, bytes_accessed=2**20, transcendentals=rows * rows
        ),
        name="self_attention",
    )(place, q, kv, hi, lo)


def visit(refs, q, keys, values, acc, top):
    at = 0
    for ref in refs:
        n = ref.shape[0]
        keys[at : at + n, :] = ref[:, :HD]
        values[at : at + n, :HD] = ref[:, HD:]
        at += n
    for t in range(q.shape[0] // TILE):
        rows = slice(t * TILE, t * TILE + TILE)
        s = dot_t(q[rows, :], keys[...])
        old = top[rows, :1]
        new = jnp.maximum(old, jnp.max(s, axis=1, keepdims=True))
        p = jnp.exp2(s - new).astype(jnp.bfloat16)
        acc[rows, :] = acc[rows, :] * jnp.exp2(old - new) + jnp.dot(
            p, values[...], preferred_element_type=jnp.float32
        )
        top[rows, :] = jnp.broadcast_to(new, (TILE, 128))


def sees(order_ref, s_ref, dh, dx):
    x, h = s_ref[4], s_ref[0]
    mine = order_ref[x * NH + (h ^ dh)]
    return order_ref[((x + dx) % NX) * NH + h] <= mine


def near_kernel(counts, order_ref, s_ref, qa_ref, qb_ref, *refs):
    blocks, (acc_ref, top_ref, q, keys, values) = refs[: sum(counts)], refs[sum(counts) :]
    dh = pl.program_id(0)
    q[...] = jnp.where(dh == 0, qa_ref[...], qb_ref[...])
    values[:, HD:] = jnp.ones((values.shape[0], HD), jnp.bfloat16)
    acc_ref[...] = jnp.zeros_like(acc_ref)
    top_ref[...] = jnp.full_like(top_ref, -NEG_LARGE)
    at = 0
    for count, dx in zip(counts, (0, NX - 1, 1)):
        unit = blocks[at : at + count]
        at += count
        pl.when(sees(order_ref, s_ref, dh, dx))(
            functools.partial(visit, unit, q, keys, values, acc_ref.at[0], top_ref.at[0])
        )


def far_kernel(order_ref, s_ref, qa_ref, qb_ref, acc_in, top_in, *refs):
    blocks, (o_ref, q, keys, values, acc, top) = refs[:-6], refs[-6:]
    dh = pl.program_id(0)
    q[...] = jnp.where(dh == 0, qa_ref[...], qb_ref[...])
    values[:, HD:] = jnp.ones((values.shape[0], HD), jnp.bfloat16)
    acc[...] = acc_in[0]
    top[...] = top_in[0]
    pl.when(sees(order_ref, s_ref, dh, 2))(
        functools.partial(visit, blocks, q, keys, values, acc, top)
    )
    y, core = s_ref[1], s_ref[3]
    for quarter in range(4):
        rows = slice(quarter * QUARTER, quarter * QUARTER + QUARTER)
        total = acc[rows, HD:]
        some = total > 0.0
        safe = jnp.where(some, total, 1.0)
        at = quarter ^ (y * 2 + core)
        o_ref[at, :QUARTER, :] = (acc[rows, :HD] / safe).astype(jnp.bfloat16)
        lse = jnp.where(some, top[rows, :] + jnp.log2(safe), -NEG_LARGE)
        row = lse.T[0:1, :]
        row = jnp.concatenate([row[:, :128], row[:, 128:]], axis=0)
        hi = row.astype(jnp.bfloat16).astype(jnp.float32)
        rest = row - hi
        mid = rest.astype(jnp.bfloat16).astype(jnp.float32)
        pad = jnp.zeros((TAIL - 6, 128), jnp.float32)
        o_ref[at, QUARTER:, :] = jnp.concatenate([hi, mid, rest - mid, pad], axis=0).astype(
            jnp.bfloat16
        )


def whole(a):
    return pl.BlockSpec(a.shape, lambda i, *s: (0,) * a.ndim)


def attention_cost(units, rows):
    pairs = 2 * units * rows * rows
    return pl.CostEstimate(flops=6 * pairs * HD, bytes_accessed=4 * 2**20, transcendentals=pairs)


def near_attention(order, place, qa, qb, units):
    rows = qa.shape[0]
    blocks = [b for unit in units for b in unit]
    out = lambda cols: pl.BlockSpec((1, rows, cols), lambda i, *s: (i, 0, 0))
    return pl.pallas_call(
        functools.partial(near_kernel, [len(unit) for unit in units]),
        grid_spec=pltpu.PrefetchScalarGridSpec(
            num_scalar_prefetch=2,
            grid=(NH,),
            in_specs=[whole(a) for a in (qa, qb, *blocks)],
            out_specs=[out(2 * HD), out(128)],
            scratch_shapes=[
                pltpu.VMEM((rows, HD), jnp.bfloat16),
                pltpu.VMEM((rows, HD), jnp.bfloat16),
                pltpu.VMEM((rows, 2 * HD), jnp.bfloat16),
            ],
        ),
        out_shape=[
            jax.ShapeDtypeStruct((NH, rows, 2 * HD), jnp.float32),
            jax.ShapeDtypeStruct((NH, rows, 128), jnp.float32),
        ],
        compiler_params=pltpu.CompilerParams(vmem_limit_bytes=VMEM_LIMIT),
        cost_estimate=attention_cost(3, rows),
        name="near_attention",
    )(order, place, qa, qb, *blocks)


def far_attention(order, place, qa, qb, acc, top, blocks):
    rows = qa.shape[0]
    chunk = QUARTER + TAIL
    part = lambda a: pl.BlockSpec((1,) + a.shape[1:], lambda i, *s: (i, 0, 0))
    return pl.pallas_call(
        far_kernel,
        grid_spec=pltpu.PrefetchScalarGridSpec(
            num_scalar_prefetch=2,
            grid=(NH,),
            in_specs=[whole(qa), whole(qb), part(acc), part(top)] + [whole(b) for b in blocks],
            out_specs=pl.BlockSpec((4, chunk, HD), lambda i, o, s: (i ^ s[0], 0, 0)),
            scratch_shapes=[
                pltpu.VMEM((rows, HD), jnp.bfloat16),
                pltpu.VMEM((rows, HD), jnp.bfloat16),
                pltpu.VMEM((rows, 2 * HD), jnp.bfloat16),
                pltpu.VMEM((rows, 2 * HD), jnp.float32),
                pltpu.VMEM((rows, 128), jnp.float32),
            ],
        ),
        out_shape=jax.ShapeDtypeStruct((NH * 4, chunk, HD), jnp.bfloat16),
        compiler_params=pltpu.CompilerParams(vmem_limit_bytes=VMEM_LIMIT),
        cost_estimate=attention_cost(1, rows),
        name="far_attention",
    )(order, place, qa, qb, acc, top, *blocks)


def join_kernel(s_ref, in_ref, near_ref, far_ref, o_ref, a_ref):
    h, y, z, core = s_ref[0], s_ref[1], s_ref[2], s_ref[3]
    place = h * 4 + y * 2 + core

    @pl.when(pl.program_id(0) == 0)
    def _():
        for r in range(4):
            parts = []
            for dh in range(NH):
                at = (dh * 4 + r) ^ place
                rows = in_ref[at, QUARTER:, :].astype(jnp.float32)
                parts.append((at, rows[0:2] + rows[2:4] + rows[4:6]))
            top = jnp.maximum(parts[0][1], parts[1][1])
            e = [jnp.exp2(lse - top) for _, lse in parts]
            norm = e[0] + e[1]
            for half in range(2):
                out = None
                for (at, _), weight in zip(parts, e):
                    w = (weight / norm)[half : half + 1, :]
                    col = jnp.broadcast_to(w, (128, 128)).T
                    term = in_ref[at, half * 128 : half * 128 + 128, :].astype(jnp.float32) * col
                    out = term if out is None else out + term
                out = out.astype(jnp.bfloat16)
                for j in range(4):
                    start = pl.multiple_of(((z + half * 4 + j) % NZ) * BLK, BLK)
                    a_ref[pl.ds(start, BLK), r * HD : r * HD + HD] = out[j * BLK : j * BLK + BLK]

    o_ref[...] = (
        jnp.dot(a_ref[:, : 2 * HD], near_ref[...], preferred_element_type=jnp.float32)
        + jnp.dot(a_ref[:, 2 * HD :], far_ref[...], preferred_element_type=jnp.float32)
    ).astype(jnp.bfloat16)


def join_heads(place, received, near, far):
    width = near.shape[1]
    step = width // 4
    cut = pl.BlockSpec((2 * HD, step), lambda i, s: (0, i))
    return pl.pallas_call(
        join_kernel,
        grid_spec=pltpu.PrefetchScalarGridSpec(
            num_scalar_prefetch=1,
            grid=(4,),
            in_specs=[whole(received), cut, cut],
            out_specs=pl.BlockSpec((QUARTER, step), lambda i, s: (0, i)),
            scratch_shapes=[pltpu.VMEM((QUARTER, 4 * HD), jnp.bfloat16)],
        ),
        out_shape=jax.ShapeDtypeStruct((QUARTER, width), jnp.bfloat16),
        compiler_params=pltpu.CompilerParams(vmem_limit_bytes=VMEM_LIMIT),
        name="join_heads",
    )(place, received, near, far)


def decode(latents, root_kernel):
    seq_count = latents.shape[0]
    row_patches = seq_count // FR
    me = lax.axis_index("seq")
    ringed = jnp.concatenate([latents[-1:], latents, latents[:1]], axis=0)
    position = (me - row_patches // 2 + seq_count) % seq_count
    patch_row = position % row_patches
    frame_index = position // row_patches
    row_ids = jnp.arange(P_SIZE + 2, dtype=jnp.int32)
    keep = jnp.where(
        row_ids == 0,
        patch_row > 0,
        jnp.where(row_ids == P_SIZE + 1, patch_row < row_patches - 1, True),
    )
    width_cols = BLK * P_SIZE
    windows = []
    for lag in range(3):
        start = (me - lag * row_patches + seq_count) % seq_count
        three = lax.dynamic_slice_in_dim(ringed, start, 3, axis=0)
        slab = (
            three.reshape(3, BLK, P_SIZE, P_SIZE, C)
            .transpose(0, 2, 1, 3, 4)
            .reshape(3 * P_SIZE, width_cols, C)
        )[P_SIZE - 1 : 2 * P_SIZE + 1]
        ok = keep & (frame_index >= lag)
        slab = jnp.where(ok[:, None, None], slab, jnp.zeros_like(slab))
        framed = jnp.pad(slab, ((0, 0), (1, 1), (0, 0)))
        for row_off in range(3):
            for col_off in range(3):
                windows.append(framed[row_off : row_off + P_SIZE, col_off : col_off + width_cols])
    stacked = jnp.concatenate(windows, axis=-1).reshape(P_SIZE * width_cols, 27 * C)
    decoded = jnp.dot(stacked, root_kernel, preferred_element_type=jnp.float32)
    return decoded.reshape(P_SIZE, width_cols, root_kernel.shape[1]).astype(jnp.bfloat16)[None]


def per_device(
    hidden, levels, span_order, modulation, in_weight, out_weight, latent_weight, decoder_weight
):
    span_me = lax.axis_index("span")
    seq_me = lax.axis_index("seq")
    x, h = span_me // NH, span_me % NH
    y, z, core = seq_me // (NZ * NC), (seq_me // NC) % NZ, seq_me % NC
    place = jnp.stack([h, y, z, core, x])
    pv = latent_weight.shape[1]
    seq_count = NY * NZ * NC

    normed, gate_row = normalize(levels, hidden[0], modulation)
    w_own = in_weight[0]
    own_blocks, other_blocks = gather_class(normed)
    w_oth = move_core(w_own)
    out_w = jnp.where(seq_me < HEADS, out_weight[0], jnp.zeros_like(out_weight[0]))
    pair = jnp.concatenate([out_w, move_core(out_w)], axis=0)
    head_latent = jnp.dot(
        out_w.astype(jnp.float32) * gate_row,
        latent_weight.astype(jnp.float32),
        precision=lax.Precision.HIGH,
    )
    latent_hi = head_latent.astype(jnp.bfloat16)
    latent_lo = (head_latent - latent_hi.astype(jnp.float32)).astype(jnp.bfloat16)
    own_latents = jnp.dot(hidden[0], latent_weight, preferred_element_type=jnp.float32)

    mine_a, theirs_a = project(own_blocks, w_own, w_oth)
    mine_b, theirs_b = project(other_blocks, w_own, w_oth)
    triples = jnp.concatenate([mine_a, move_core(theirs_a), mine_b, move_core(theirs_b)], axis=0)
    q = triples[:, :HD]
    kv = triples[:, HD:]

    half = kv.shape[0] // 2
    kv_up, kv_dn = move_x(kv, 1), move_x(kv, -1)
    q_hi = move_hi(q)
    kv_far = (move_x(kv_up[:half], 1), move_x(kv_dn[half:], -1))

    far_pair = move_y(lax.optimization_barrier((pair, other_blocks[4]))[0])

    part = self_attention(place, q, kv, latent_hi, latent_lo)
    q_hi, part = lax.optimization_barrier((q_hi, part))
    acc, top = near_attention(span_order, place, q, q_hi, ((kv,), (kv_up,), (kv_dn,)))
    part = lax.all_to_all(part, "seq", 0, 0, tiled=True)
    acc, part = lax.optimization_barrier((acc, part))
    chunks = far_attention(span_order, place, q, q_hi, acc, top, kv_far)
    groups = [
        [
            span_at(i, hh) * seq_count + seq_at(yy, j, cc)
            for hh in range(NH)
            for yy in range(NY)
            for cc in range(NC)
        ]
        for i in range(NX)
        for j in range(NZ)
    ]
    received = lax.all_to_all(
        chunks, ("span", "seq"), 0, 0, tiled=True, axis_index_groups=groups
    )
    partial = join_heads(place, received, pair, far_pair)
    z_groups = [[seq_at(yy, j, cc) for j in range(NZ)] for yy in range(NY) for cc in range(NC)]
    summed = lax.psum_scatter(
        partial, "seq", scatter_dimension=0, tiled=True, axis_index_groups=z_groups
    ).astype(jnp.float32)
    block_out = (hidden[0].astype(jnp.float32) + gate_row * summed).astype(jnp.bfloat16)[None]

    latents = (jnp.sum(part.astype(jnp.float32), axis=0) + own_latents).astype(jnp.bfloat16)
    group_ids = jnp.arange(span_order.shape[0], dtype=jnp.int32)
    root = jnp.sum(jnp.where(span_order == 0, group_ids, 0))
    spread = lax.all_to_all(
        jnp.broadcast_to(latents[None], (NX * NH, BLK, pv)), "span", 0, 0, tiled=True
    )
    latents = lax.dynamic_index_in_dim(spread, root, 0, keepdims=True)
    every = lax.all_to_all(
        jnp.broadcast_to(latents, (seq_count, BLK, pv)), "seq", 0, 0, tiled=True
    )
    decoded = decode(every, decoder_weight.reshape(27 * C, decoder_weight.shape[4]))
    return (block_out, decoded)


def solution(mesh):
    placed = (
        P("span", "seq", None),
        P("span"),
        P(),
        P(),
        P("seq", None, None),
        P("seq", None, None),
        P(),
        P(None, None, None, None, "span"),
    )
    return jax.shard_map(
        per_device,
        mesh=mesh,
        in_specs=placed,
        out_specs=(P("span", "seq", None), P("seq", None, None, "span")),
        check_vma=False,
    )
```

time: 220 us -> 207 us (0.941)
  starting transfers between devices: 60.9 us -> 41.5 us
  waiting for transfers between devices: 58.3 us -> 77.3 us
  Pallas kernels: 17.3 us -> 32.2 us
  matrix products: 13.6 us -> 3.44 us
  between operations: 26 us -> 17.1 us
  local copies, waits for them, and re-layouts: 13.7 us -> 9.21 us
  other arithmetic: 11.2 us -> 7.48 us
    ppermute x1, waiting for transfers between devices: 0.01 us -> 24 us  [move_hi(): return lax.ppermute(a, 'span', span_route(dh=1))]
    all_to_all x1, starting transfers between devices: 17.8 us -> 4.99 us  [per_device(): lax.all_to_all(chunks, ('span', 'seq'), 0, 0, tiled=True, axis_index_grou...]
    pallas_call x2 -> x6, Pallas kernels: 14.5 us -> 26.6 us  [the longest x1 7.94 us: near_attention(): pl.pallas_call(functools.partial(near_kernel, [len(unit) for unit in unit...]
    dot_general x6 -> x1, matrix products: 12.6 us -> 2.42 us  [per_device(): jnp.dot(out_w.astype(jnp.float32) * gate_row, latent_weight.astype(jnp.fl...]
    ppermute x4, waiting for transfers between devices: 9.1 us -> 0.01 us  [move_x(): return lax.ppermute(a, 'span', span_route(dx=d))]
    reduce_scatter x1, waiting for transfers between devices: 0.01 us -> 7.99 us  [per_device(): lax.psum_scatter(partial, 'seq', scatter_dimension=0, tiled=True, axis_in...]
    ppermute x12 -> x9, waiting for transfers between devices: 26.4 us -> 18.5 us  [move_z(): return lax.ppermute(a, 'seq', seq_route(dz=d))]
    unnamed x50 -> x27, local copies, waits for them, and re-layouts: 10.8 us -> 5.42 us
  transfers between devices with their start and end apart: 30 -> 29, of which waited for: 12 -> 14; matrix products, arithmetic and copies ran while one was open for 13% -> 9% of each run, Pallas kernels for 8% -> 13%
where the time goes in v2:
time: 207 us; the launch traced here: 205 us
  waiting for transfers between devices  77.3 us (37%)
  starting transfers between devices  41.5 us (20%)
  Pallas kernels  32.2 us (16%)
  between operations  17.1 us (8%)
  blocking collectives  16.7 us (8%)
  local copies, waits for them, and re-layouts  9.21 us (4%)
  other arithmetic  7.48 us (4%)
  matrix products  3.44 us (2%)
    ppermute x1, waiting for transfers between devices, move_hi(): return lax.ppermute(a, 'span', span_route(dh=1))  24 us
    ppermute x9, waiting for transfers between devices, move_z(): return lax.ppermute(a, 'seq', seq_route(dz=d))  18.5 us
    all_to_all x1, blocking collectives, per_device(): part = lax.all_to_all(part, 'seq', 0, 0, tiled=True)  16.7 us
    ppermute x9, starting transfers between devices, move_z(): return lax.ppermute(a, 'seq', seq_route(dz=d))  14.6 us
    all_to_all x1, waiting for transfers between devices, per_device(): lax.all_to_all(chunks, ('span', 'seq'), 0, 0, tiled=True, axis_index_grou...  9.26 us
    all_to_all x1, waiting for transfers between devices, per_device(): lax.all_to_all(jnp.broadcast_to(latents, (seq_count, BLK, pv)), 'seq', 0,...  8.98 us
    reduce_scatter x1, waiting for transfers between devices, per_device(): lax.psum_scatter(partial, 'seq', scatter_dimension=0, tiled=True, axis_in...  7.99 us
    pallas_call x1, Pallas kernels, near_attention(): pl.pallas_call(functools.partial(near_kernel, [len(unit) for unit in unit...  7.94 us
  transfers between devices with their start and end apart: 29, of which 14 were waited for; matrix products, arithmetic and copies ran while one was open for 9% of the time, Pallas kernels for 13%

profile of v2, /device:TPU:10, one launch (start us, length us, event | category | flops | bytes accessed | tf_op | source)
XLA Modules:
  0.0 204.9 jit_solution(7162565335579406142)
XLA Ops:
  8.0 2.4 %copy.32.mod_ref = f32[16,3,3072]{2,1,0:T(4,128)} copy(f32[16,3,3072]{2,0,1:T(8,128)} %param.11) | data formatting | bytes 1179648 | tf_op args[3]
  10.3 1.9 normalize.1
  12.2 1.9 collective-permute-start.3
  14.2 4.0 %collective-permute-start = (bf16[32,3072]{1,0:T(8,128)(2,1)}, bf16[32,3072]{1,0:T(8,128)(2,1)S(1)}, u32[]{:S(2)}, u32[]{:S(2)}) collective-permute-start(bf16[32,3072]{1,0:T(8,128)(2,1)} %get-tuple-element.16.refs_0_), channel_id=1, source_target_pairs={{0,14},{1,15},{2,0},{3,1},{4,2},{5,3},{6,4},{7,5},{8,6},{9,7},{10,... | collective-permute-start | bytes 589832 | tf_op jit(solution)/shard_map/ppermute | solution.py:48
  18.2 5.7 %collective-permute-done.3.refs_7_ = bf16[32,3072]{1,0:T(8,128)(2,1)S(1)} collective-permute-done((bf16[32,3072]{1,0:T(8,128)(2,1)}, bf16[32,3072]{1,0:T(8,128)(2,1)S(1)}, u32[]{:S(2)}, u32[]{:S(2)}) %collective-permute-start.3) | collective-permute-done | bytes 196640 | tf_op jit(solution)/shard_map/ppermute | solution.py:48
  23.9 2.1 %select_bitcast_fusion = bf16[128,3072]{1,0:T(8,128)(2,1)} fusion(bf16[1,128,3072]{2,1,0:T(8,128)(2,1)} %param.13, pred[]{:T(512)S(6)} %lt.56), kind=kLoop, calls=%fused_computation.9 | loop fusion | flops 393216 | bytes 1572865 | tf_op jit(solution)/shard_map/jit(_where)/select_n | solution.py:429
  26.0 2.1 %collective-permute-start.1 = (bf16[32,3072]{1,0:T(8,128)(2,1)S(1)}, bf16[32,3072]{1,0:T(8,128)(2,1)}, u32[]{:S(2)}, u32[]{:S(2)}) collective-permute-start(bf16[32,3072]{1,0:T(8,128)(2,1)S(1)} %collective-permute-done.refs_1_), channel_id=1, source_target_pairs={{0,14},{1,15},{2,0},{3,1},{4,2},{5,3},{6,4},{7,5},{8,6},{9,7},{10,... | collective-permute-start | bytes 589832 | tf_op jit(solution)/shard_map/ppermute | solution.py:48
  28.1 3.7 %collective-permute-done.4.refs_6_ = bf16[32,3072]{1,0:T(8,128)(2,1)S(1)} collective-permute-done((bf16[32,3072]{1,0:T(8,128)(2,1)S(1)}, bf16[32,3072]{1,0:T(8,128)(2,1)S(1)}, u32[]{:S(2)}, u32[]{:S(2)}) %collective-permute-start.4) | collective-permute-done | bytes 196640 | tf_op jit(solution)/shard_map/ppermute | solution.py:48
  31.8 1.6 collective-permute-done.1.refs_2_
  33.4 3.3 %collective-permute-start.2 = (bf16[32,3072]{1,0:T(8,128)(2,1)}, bf16[32,3072]{1,0:T(8,128)(2,1)}, u32[]{:S(2)}, u32[]{:S(2)}) collective-permute-start(bf16[32,3072]{1,0:T(8,128)(2,1)} %collective-permute-done.1.refs_2_), channel_id=1, source_target_pairs={{0,14},{1,15},{2,0},{3,1},{4,2},{5,3},{6,4},{7,5},{8,6},{9,7},{10,... | collective-permute-start | bytes 589832 | tf_op jit(solution)/shard_map/ppermute | solution.py:48
  36.7 2.2 %collective-permute-done.5.refs_5_ = bf16[32,3072]{1,0:T(8,128)(2,1)} collective-permute-done((bf16[32,3072]{1,0:T(8,128)(2,1)S(1)}, bf16[32,3072]{1,0:T(8,128)(2,1)}, u32[]{:S(2)}, u32[]{:S(2)}) %collective-permute-start.5) | collective-permute-done | bytes 196640 | tf_op jit(solution)/shard_map/ppermute | solution.py:48
  39.0 0.5 collective-permute-start.11
  39.4 1.7 collective-permute-done.2.refs_3_
  41.1 1.6 collective-permute-start.14
  42.7 3.5 %collective-permute-done.6.refs_4_ = bf16[32,3072]{1,0:T(8,128)(2,1)} collective-permute-done((bf16[32,3072]{1,0:T(8,128)(2,1)}, bf16[32,3072]{1,0:T(8,128)(2,1)}, u32[]{:S(2)}, u32[]{:S(2)}) %collective-permute-start.6) | collective-permute-done | bytes 196640 | tf_op jit(solution)/shard_map/ppermute | solution.py:48
  46.2 0.4 collective-permute-start.13
  46.6 2.4 %fusion.10 = (bf16[128,64]{0,1:T(8,128)(2,1)S(1)}, f32[128,64]{0,1:T(8,128)}) fusion(bf16[3072,64]{0,1:T(8,128)(2,1)S(1)} %copy-done, bf16[128,3072]{1,0:T(8,128)(2,1)} %select_bitcast_fusion, f32[3072]{0:T(1024)} %bitcast.49), kind=kOutput, calls=%fused_computation.52 | convolution fusion | flops 151789568 | bytes 1241088 | tf_op jit(solution)/shard_map/dot_general | solution.py:431
  49.0 0.7 copy.35.hi_ref
  49.7 1.5 copy.34
  51.3 1.7 collective-permute-start.9
  53.0 0.5 collective-permute-start.10
  53.4 1.6 collective-permute-start.16
  55.0 0.2 collective-permute-done.13.refs_4_
  55.3 3.2 %collective-permute-start.12 = (bf16[32,3072]{1,0:T(8,128)(2,1)}, bf16[32,3072]{1,0:T(8,128)(2,1)S(1)}, u32[]{:S(2)}, u32[]{:S(2)}) collective-permute-start(bf16[32,3072]{1,0:T(8,128)(2,1)} %collective-permute-done.11.refs_2_), channel_id=1, source_target_pairs={{0,14},{1,15},{2,0},{3,1},{4,2},{5,3},{6,4},{7,5},{8,6},{9,7},{10,... | collective-permute-start | bytes 589832 | tf_op jit(solution)/shard_map/ppermute | solution.py:48
  58.5 2.6 %pad_maximum_fusion.near_ref = bf16[256,3072]{1,0:T(8,128)(2,1)} fusion(bf16[128,3072]{1,0:T(8,128)(2,1)} %collective-permute-done.23, bf16[128,3072]{1,0:T(8,128)(2,1)} %select_bitcast_fusion), kind=kLoop, calls=%fused_computation | loop fusion | flops 3145728 | bytes 3145728 | tf_op jit(solution)/shard_map/concatenate | solution.py:430
  61.1 3.0 %project.2 = (bf16[256,384]{1,0:T(8,128)(2,1)S(1)}, bf16[256,384]{1,0:T(8,128)(2,1)S(1)}) custom-call(bf16[32,3072]{1,0:T(8,128)(2,1)S(1)} %copy-done.2, bf16[32,3072]{1,0:T(8,128)(2,1)S(1)} %collective-permute-done.refs_1_, bf16[32,3072]{1,0:T(8,128)(2,1)} %collective-permute-done.1.refs_2_, bf16[32,3072]{1,0:T(8,128)(2,1)} %collective-permute-done.2.refs_3_, ...), custom_call_target="tpu_custom_call" | custom-call | flops 1207959552 | bytes 6291456 | tf_op jit(solution)/shard_map/project/pallas_call | solution.py:130
  64.2 0.1 collective-permute-start.24
  64.4 3.4 %collective-permute-done.16.refs_7_ = bf16[32,3072]{1,0:T(8,128)(2,1)S(1)} collective-permute-done((bf16[32,3072]{1,0:T(8,128)(2,1)S(1)}, bf16[32,3072]{1,0:T(8,128)(2,1)S(1)}, u32[]{:S(2)}, u32[]{:S(2)}) %collective-permute-start.16) | collective-permute-done | bytes 196640 | tf_op jit(solution)/shard_map/ppermute | solution.py:52
  67.8 2.9 %project.3 = (bf16[256,384]{1,0:T(8,128)(2,1)S(1)}, bf16[256,384]{1,0:T(8,128)(2,1)S(1)}) custom-call(bf16[32,3072]{1,0:T(8,128)(2,1)S(1)} %collective-permute-done.9.refs_0_, bf16[32,3072]{1,0:T(8,128)(2,1)S(1)} %collective-permute-done.10.refs_1_, bf16[32,3072]{1,0:T(8,128)(2,1)} %collective-permute-done.11.refs_2_, ...), custom_call_target="tpu_custom_call" | custom-call | flops 1207959552 | bytes 6291456 | tf_op jit(solution)/shard_map/project/pallas_call | solution.py:130
  71.0 1.3 collective-permute-done.17
  72.4 1.6 collective-permute-start.19
  73.9 0.5 collective-permute-start.20
  74.5 2.5 %collective-permute-start.18 = (bf16[1024,128]{1,0:T(8,128)(2,1)S(1)}, bf16[1024,128]{1,0:T(8,128)(2,1)S(1)}, u32[]{:S(2)}, u32[]{:S(2)}) collective-permute-start(bf16[1024,128]{1,0:T(8,128)(2,1)S(1)} %slice.153.q_ref.qa_ref), channel_id=1, source_target_pairs={{0,32},{32,0},{64,96},{96,64},{128,160},{160,128},{192,224},{224,1... | collective-permute-start | bytes 786440 | tf_op jit(solution)/shard_map/ppermute | solution.py:64
  76.9 5.3 %self_attention.1 = bf16[32,32,64]{2,1,0:T(8,128)(2,1)S(1)} custom-call(s32[5]{0:T(128)S(1)} %stack.23.s_ref, bf16[1024,128]{1,0:T(8,128)(2,1)S(1)} %slice.153.q_ref.qa_ref, bf16[1024,256]{1,0:T(8,128)(2,1)S(1)} %slice.154.kv_ref.refs_0_, bf16[128,64]{1,0:T(8,128)(2,1)S(1)} %copy-done.3, bf16[128,64]{1,0:T(8,128)(2,1)S(1)} %subtract_convert_fusion.lo_ref), custom_call_target="tpu_custom_call" | custom-call | flops 805306368 | bytes 1048576 | tf_op jit(solution)/shard_map/self_attention/pallas_call | solution.py:176
  82.3 24.0 %collective-permute-done.18.qb_ref = bf16[1024,128]{1,0:T(8,128)(2,1)S(1)} collective-permute-done((bf16[1024,128]{1,0:T(8,128)(2,1)S(1)}, bf16[1024,128]{1,0:T(8,128)(2,1)S(1)}, u32[]{:S(2)}, u32[]{:S(2)}) %collective-permute-start.18) | collective-permute-done | bytes 262176 | tf_op jit(solution)/shard_map/ppermute | solution.py:64
  106.2 0.2 reshape.56
  106.4 16.7 %all_to_all.20 = bf16[32,2,1024]{2,1,0:T(2,128)(2,1)S(1)} all-to-all(bf16[32,2,1024]{2,1,0:T(2,128)(2,1)S(1)} %reshape.56), channel_id=1, replica_groups=mesh['span'=8,'seq'=32] {'seq'}, dimensions={0} | all-to-all | bytes 262144 | tf_op jit(solution)/shard_map/all_to_all | solution.py:456
  123.1 0.2 reshape.57
  123.4 1.8 collective-permute-start.21
  125.2 0.6 collective-permute-start.22
  125.8 7.9 %near_attention.1 = (f32[2,1024,256]{2,1,0:T(8,128)S(1)}, f32[2,1024,128]{2,1,0:T(8,128)S(1)}) custom-call(s32[8]{0:T(128)S(1)} %copy-done.4, s32[5]{0:T(128)S(1)} %stack.23.s_ref, bf16[1024,128]{1,0:T(8,128)(2,1)S(1)} %slice.153.q_ref.qa_ref, bf16[1024,128]{1,0:T(8,128)(2,1)S(1)} %collective-permute-done.18.qb_ref, ...), custom_call_target="tpu_custom_call" | custom-call | flops 4831838208 | bytes 4194304 | tf_op jit(solution)/shard_map/near_attention/pallas_call | solution.py:278
  133.8 5.5 %far_attention.1 = bf16[8,272,128]{2,1,0:T(8,128)(2,1)} custom-call(s32[8]{0:T(128)S(1)} %copy-done.4, s32[5]{0:T(128)S(1)} %stack.23.s_ref, bf16[1024,128]{1,0:T(8,128)(2,1)S(1)} %slice.153.q_ref.qa_ref, bf16[1024,128]{1,0:T(8,128)(2,1)S(1)} %collective-permute-done.18.qb_ref, f32[2,1024,256]{2,1,0:T(8,128)S(1)} %get-tuple-element.24.acc_in, ...), custom_call_target="tpu_custom_call" | custom-call | flops 1610612736 | bytes 4194304 | tf_op jit(solution)/shard_map/far_attention/pallas_call | solution.py:305
  139.3 5.0 %all-to-all-start.1 = ((bf16[8,272,128]{2,1,0:T(8,128)(2,1)}), bf16[8,272,128]{2,1,0:T(8,128)(2,1)S(1)}, u32[]{:S(2)}, u32[]{:S(2)}) async-start(bf16[8,272,128]{2,1,0:T(8,128)(2,1)} %far_attention.1), calls=%async_computation.1 | async-start | bytes 1114112 | tf_op jit(solution)/shard_map/all_to_all | solution.py:469
  144.3 9.3 %all-to-all-done.1.in_ref = bf16[8,272,128]{2,1,0:T(8,128)(2,1)S(1)} async-done(((bf16[8,272,128]{2,1,0:T(8,128)(2,1)}), bf16[8,272,128]{2,1,0:T(8,128)(2,1)S(1)}, u32[]{:S(2)}, u32[]{:S(2)}) %all-to-all-start.1) | async-done | bytes 557088 | tf_op jit(solution)/shard_map/all_to_all | solution.py:469
  153.5 5.6 %join_heads.1 = bf16[256,3072]{1,0:T(8,128)(2,1)} custom-call(s32[5]{0:T(128)S(1)} %stack.23.s_ref, bf16[8,272,128]{2,1,0:T(8,128)(2,1)S(1)} %all-to-all-done.1.in_ref, bf16[256,3072]{1,0:T(8,128)(2,1)} %pad_maximum_fusion.near_ref, bf16[256,3072]{1,0:T(8,128)(2,1)} %collective-permute-done.24.far_ref), custom_call_target="tpu_custom_call" | custom-call | tf_op jit(solution)/shard_map/join_heads/pallas_call | solution.py:364
  159.2 0.8 copy-done.5
  160.0 0.2 fusion.4
  160.3 0.7 reshape.58
  161.0 4.2 %all-to-all-start.2 = ((bf16[8,2,1024]{2,1,0:T(2,128)(2,1)}), bf16[8,2,1024]{2,1,0:T(2,128)(2,1)S(1)}, u32[]{:S(2)}, u32[]{:S(2)}) async-start(bf16[8,2,1024]{2,1,0:T(2,128)(2,1)} %reshape.58), calls=%async_computation.3 | async-start | bytes 65536 | tf_op jit(solution)/shard_map/all_to_all | solution.py:482
  165.2 0.6 fusion.7
  167.8 3.7 %all-to-all-done.2 = bf16[8,2,1024]{2,1,0:T(2,128)(2,1)S(1)} async-done(((bf16[8,2,1024]{2,1,0:T(2,128)(2,1)}), bf16[8,2,1024]{2,1,0:T(2,128)(2,1)S(1)}, u32[]{:S(2)}, u32[]{:S(2)}) %all-to-all-start.2) | async-done | bytes 32800 | tf_op jit(solution)/shard_map/all_to_all | solution.py:482
  171.6 0.8 reshape.60
  172.5 4.2 %all-to-all-start.3 = ((bf16[32,2,1024]{2,1,0:T(2,128)(2,1)}), bf16[32,2,1024]{2,1,0:T(2,128)(2,1)S(1)}, u32[]{:S(2)}, u32[]{:S(2)}) async-start(bf16[32,2,1024]{2,1,0:T(2,128)(2,1)} %reshape.60), calls=%async_computation.4 | async-start | bytes 262144 | tf_op jit(solution)/shard_map/all_to_all | solution.py:486
  176.8 9.0 %all-to-all-done.3 = bf16[32,2,1024]{2,1,0:T(2,128)(2,1)S(1)} async-done(((bf16[32,2,1024]{2,1,0:T(2,128)(2,1)}), bf16[32,2,1024]{2,1,0:T(2,128)(2,1)S(1)}, u32[]{:S(2)}, u32[]{:S(2)}) %all-to-all-start.3) | async-done | bytes 131104 | tf_op jit(solution)/shard_map/all_to_all | solution.py:486
  185.8 0.2 reshape.61
  186.0 0.3 copy.36
  186.3 0.1 pad_maximum_fusion.1
  186.5 0.1 copy.39
  186.6 0.1 copy.40
  186.7 0.1 copy.41
  187.2 0.3 concatenate.15
  187.6 0.8 fusion.3
  188.4 8.0 %reduce-scatter.2.cloned.1.call-done = bf16[32,3072]{1,0:T(8,128)(2,1)} async-done(((bf16[256,3072]{1,0:T(8,128)(2,1)}), bf16[32,3072]{1,0:T(8,128)(2,1)}) %reduce-scatter.2.cloned.1.call-update) | async-done | bytes 196624 | tf_op jit(solution)/shard_map/reduce_scatter | solution.py:474
  196.4 1.7 fusion.6
  (67 shorter events, 1.3 us)
Async XLA Ops:
  7.2 39.4 %copy-start = (bf16[3072,64]{0,1:T(8,128)(2,1)S(1)}, bf16[3072,64]{0,1:T(8,128)(2,1)}, u32[]{:S(2)}) copy-start(bf16[3072,64]{0,1:T(8,128)(2,1)} %param.14) | copy-start | bytes 1179652
  7.2 51.3 %collective-permute-start.7 = (bf16[3072,384]{1,0:T(8,128)(2,1)}, bf16[3072,384]{1,0:T(8,128)(2,1)S(1)}, u32[]{:S(2)}, u32[]{:S(2)}) collective-permute-start(bf16[3072,384]{1,0:T(8,128)(2,1)} %bitcast.38), channel_id=1, source_target_pairs={{0,1},{1,0},{2,3},{3,2},{4,5},{5,4},{6,7},{7,6},{8,9},{9,8},{10,11... | collective-permute-start | bytes 7077896 | tf_op jit(solution)/shard_map/ppermute | solution.py:56
  12.2 39.1 %copy-start.2 = (bf16[32,3072]{1,0:T(8,128)(2,1)S(1)}, bf16[32,3072]{1,0:T(8,128)(2,1)}, u32[]{:S(2)}) copy-start(bf16[32,3072]{1,0:T(8,128)(2,1)} %get-tuple-element.16.refs_0_) | copy-start | bytes 589828
  12.2 11.7 %collective-permute-start.3 = (bf16[32,3072]{1,0:T(8,128)(2,1)}, bf16[32,3072]{1,0:T(8,128)(2,1)S(1)}, u32[]{:S(2)}, u32[]{:S(2)}) collective-permute-start(bf16[32,3072]{1,0:T(8,128)(2,1)} %get-tuple-element.16.refs_0_), channel_id=1, source_target_pairs={{0,2},{1,3},{2,4},{3,5},{4,6},{5,7},{6,8},{7,9},{8,10},{9,11},{10,... | collective-permute-start | bytes 589832 | tf_op jit(solution)/shard_map/ppermute | solution.py:48
  14.2 11.8 %collective-permute-start = (bf16[32,3072]{1,0:T(8,128)(2,1)}, bf16[32,3072]{1,0:T(8,128)(2,1)S(1)}, u32[]{:S(2)}, u32[]{:S(2)}) collective-permute-start(bf16[32,3072]{1,0:T(8,128)(2,1)} %get-tuple-element.16.refs_0_), channel_id=1, source_target_pairs={{0,14},{1,15},{2,0},{3,1},{4,2},{5,3},{6,4},{7,5},{8,6},{9,7},{10,... | collective-permute-start | bytes 589832 | tf_op jit(solution)/shard_map/ppermute | solution.py:48
  23.9 7.9 %collective-permute-start.4 = (bf16[32,3072]{1,0:T(8,128)(2,1)S(1)}, bf16[32,3072]{1,0:T(8,128)(2,1)S(1)}, u32[]{:S(2)}, u32[]{:S(2)}) collective-permute-start(bf16[32,3072]{1,0:T(8,128)(2,1)S(1)} %collective-permute-done.3.refs_7_), channel_id=1, source_target_pairs={{0,2},{1,3},{2,4},{3,5},{4,6},{5,7},{6,8},{7,9},{8,10},{9,11},{10,... | collective-permute-start | bytes 589832 | tf_op jit(solution)/shard_map/ppermute | solution.py:48
  26.0 27.4 %collective-permute-start.23 = (bf16[128,3072]{1,0:T(8,128)(2,1)}, bf16[128,3072]{1,0:T(8,128)(2,1)}, u32[]{:S(2)}, u32[]{:S(2)}) collective-permute-start(bf16[128,3072]{1,0:T(8,128)(2,1)} %select_bitcast_fusion), channel_id=1, source_target_pairs={{0,1},{1,0},{2,3},{3,2},{4,5},{5,4},{6,7},{7,6},{8,9},{9,8},{10,11... | collective-permute-start | bytes 2359304 | tf_op jit(solution)/shard_map/ppermute | solution.py:56
  26.0 7.4 %collective-permute-start.1 = (bf16[32,3072]{1,0:T(8,128)(2,1)S(1)}, bf16[32,3072]{1,0:T(8,128)(2,1)}, u32[]{:S(2)}, u32[]{:S(2)}) collective-permute-start(bf16[32,3072]{1,0:T(8,128)(2,1)S(1)} %collective-permute-done.refs_1_), channel_id=1, source_target_pairs={{0,14},{1,15},{2,0},{3,1},{4,2},{5,3},{6,4},{7,5},{8,6},{9,7},{10,... | collective-permute-start | bytes 589832 | tf_op jit(solution)/shard_map/ppermute | solution.py:48
  31.8 7.1 %collective-permute-start.5 = (bf16[32,3072]{1,0:T(8,128)(2,1)S(1)}, bf16[32,3072]{1,0:T(8,128)(2,1)}, u32[]{:S(2)}, u32[]{:S(2)}) collective-permute-start(bf16[32,3072]{1,0:T(8,128)(2,1)S(1)} %collective-permute-done.4.refs_6_), channel_id=1, source_target_pairs={{0,2},{1,3},{2,4},{3,5},{4,6},{5,7},{6,8},{7,9},{8,10},{9,11},{10,... | collective-permute-start | bytes 589832 | tf_op jit(solution)/shard_map/ppermute | solution.py:48
  33.4 7.7 %collective-permute-start.2 = (bf16[32,3072]{1,0:T(8,128)(2,1)}, bf16[32,3072]{1,0:T(8,128)(2,1)}, u32[]{:S(2)}, u32[]{:S(2)}) collective-permute-start(bf16[32,3072]{1,0:T(8,128)(2,1)} %collective-permute-done.1.refs_2_), channel_id=1, source_target_pairs={{0,14},{1,15},{2,0},{3,1},{4,2},{5,3},{6,4},{7,5},{8,6},{9,7},{10,... | collective-permute-start | bytes 589832 | tf_op jit(solution)/shard_map/ppermute | solution.py:48
  39.0 7.2 %collective-permute-start.6 = (bf16[32,3072]{1,0:T(8,128)(2,1)}, bf16[32,3072]{1,0:T(8,128)(2,1)}, u32[]{:S(2)}, u32[]{:S(2)}) collective-permute-start(bf16[32,3072]{1,0:T(8,128)(2,1)} %collective-permute-done.5.refs_5_), channel_id=1, source_target_pairs={{0,2},{1,3},{2,4},{3,5},{4,6},{5,7},{6,8},{7,9},{8,10},{9,11},{10,... | collective-permute-start | bytes 589832 | tf_op jit(solution)/shard_map/ppermute | solution.py:48
  39.0 12.3 %collective-permute-start.11 = (bf16[32,3072]{1,0:T(8,128)(2,1)}, bf16[32,3072]{1,0:T(8,128)(2,1)}, u32[]{:S(2)}, u32[]{:S(2)}) collective-permute-start(bf16[32,3072]{1,0:T(8,128)(2,1)} %collective-permute-done.1.refs_2_), channel_id=1, source_target_pairs={{0,16},{1,17},{2,18},{3,19},{4,20},{5,21},{6,22},{7,23},{8,24},{9,... | collective-permute-start | bytes 589832 | tf_op jit(solution)/shard_map/ppermute | solution.py:52
  41.1 11.9 %collective-permute-start.14 = (bf16[32,3072]{1,0:T(8,128)(2,1)S(1)}, bf16[32,3072]{1,0:T(8,128)(2,1)}, u32[]{:S(2)}, u32[]{:S(2)}) collective-permute-start(bf16[32,3072]{1,0:T(8,128)(2,1)S(1)} %collective-permute-done.4.refs_6_), channel_id=1, source_target_pairs={{0,16},{1,17},{2,18},{3,19},{4,20},{5,21},{6,22},{7,23},{8,24},{9,... | collective-permute-start | bytes 589832 | tf_op jit(solution)/shard_map/ppermute | solution.py:52
  46.2 9.1 %collective-permute-start.13 = (bf16[32,3072]{1,0:T(8,128)(2,1)}, bf16[32,3072]{1,0:T(8,128)(2,1)}, u32[]{:S(2)}, u32[]{:S(2)}) collective-permute-start(bf16[32,3072]{1,0:T(8,128)(2,1)} %collective-permute-done.6.refs_4_), channel_id=1, source_target_pairs={{0,16},{1,17},{2,18},{3,19},{4,20},{5,21},{6,22},{7,23},{8,24},{9,... | collective-permute-start | bytes 589832 | tf_op jit(solution)/shard_map/ppermute | solution.py:52
  51.3 9.8 %copy-start.1 = (bf16[1,3072,384]{2,1,0:T(8,128)(2,1)S(1)}, bf16[1,3072,384]{2,1,0:T(8,128)(2,1)}, u32[]{:S(2)}) copy-start(bf16[1,3072,384]{2,1,0:T(8,128)(2,1)} %param.12) | copy-start | bytes 7077892
  51.3 12.8 %collective-permute-start.9 = (bf16[32,3072]{1,0:T(8,128)(2,1)S(1)}, bf16[32,3072]{1,0:T(8,128)(2,1)S(1)}, u32[]{:S(2)}, u32[]{:S(2)}) collective-permute-start(bf16[32,3072]{1,0:T(8,128)(2,1)S(1)} %copy-done.2), channel_id=1, source_target_pairs={{0,16},{1,17},{2,18},{3,19},{4,20},{5,21},{6,22},{7,23},{8,24},{9,... | collective-permute-start | bytes 589832 | tf_op jit(solution)/shard_map/ppermute | solution.py:52
  53.0 11.3 %collective-permute-start.10 = (bf16[32,3072]{1,0:T(8,128)(2,1)S(1)}, bf16[32,3072]{1,0:T(8,128)(2,1)S(1)}, u32[]{:S(2)}, u32[]{:S(2)}) collective-permute-start(bf16[32,3072]{1,0:T(8,128)(2,1)S(1)} %collective-permute-done.refs_1_), channel_id=1, source_target_pairs={{0,16},{1,17},{2,18},{3,19},{4,20},{5,21},{6,22},{7,23},{8,24},{9,... | collective-permute-start | bytes 589832 | tf_op jit(solution)/shard_map/ppermute | solution.py:52
  53.4 14.4 %collective-permute-start.16 = (bf16[32,3072]{1,0:T(8,128)(2,1)S(1)}, bf16[32,3072]{1,0:T(8,128)(2,1)S(1)}, u32[]{:S(2)}, u32[]{:S(2)}) collective-permute-start(bf16[32,3072]{1,0:T(8,128)(2,1)S(1)} %collective-permute-done.3.refs_7_), channel_id=1, source_target_pairs={{0,16},{1,17},{2,18},{3,19},{4,20},{5,21},{6,22},{7,23},{8,24},{9,... | collective-permute-start | bytes 589832 | tf_op jit(solution)/shard_map/ppermute | solution.py:52
  55.3 12.5 %collective-permute-start.12 = (bf16[32,3072]{1,0:T(8,128)(2,1)}, bf16[32,3072]{1,0:T(8,128)(2,1)S(1)}, u32[]{:S(2)}, u32[]{:S(2)}) collective-permute-start(bf16[32,3072]{1,0:T(8,128)(2,1)} %collective-permute-done.11.refs_2_), channel_id=1, source_target_pairs={{0,14},{1,15},{2,0},{3,1},{4,2},{5,3},{6,4},{7,5},{8,6},{9,7},{10,... | collective-permute-start | bytes 589832 | tf_op jit(solution)/shard_map/ppermute | solution.py:48
  58.5 9.3 %collective-permute-start.15 = (bf16[32,3072]{1,0:T(8,128)(2,1)}, bf16[32,3072]{1,0:T(8,128)(2,1)S(1)}, u32[]{:S(2)}, u32[]{:S(2)}) collective-permute-start(bf16[32,3072]{1,0:T(8,128)(2,1)} %collective-permute-done.14.refs_6_), channel_id=1, source_target_pairs={{0,2},{1,3},{2,4},{3,5},{4,6},{5,7},{6,8},{7,9},{8,10},{9,11},{10,... | collective-permute-start | bytes 589832 | tf_op jit(solution)/shard_map/ppermute | solution.py:48
  64.2 80.1 %collective-permute-start.24 = (bf16[256,3072]{1,0:T(8,128)(2,1)}, bf16[256,3072]{1,0:T(8,128)(2,1)}, u32[]{:S(2)}, u32[]{:S(2)}) collective-permute-start(bf16[256,3072]{1,0:T(8,128)(2,1)} %pad_maximum_fusion.near_ref), channel_id=1, source_target_pairs={{0,16},{1,17},{2,18},{3,19},{4,20},{5,21},{6,22},{7,23},{8,24},{9,... | collective-permute-start | bytes 4718600 | tf_op jit(solution)/shard_map/ppermute | solution.py:52
  64.3 6.6 %collective-permute-start.8 = (bf16[256,384]{1,0:T(8,128)(2,1)S(1)}, bf16[256,384]{1,0:T(8,128)(2,1)S(1)}, u32[]{:S(2)}, u32[]{:S(2)}) collective-permute-start(bf16[256,384]{1,0:T(8,128)(2,1)S(1)} %get-tuple-element.18), channel_id=1, source_target_pairs={{0,1},{1,0},{2,3},{3,2},{4,5},{5,4},{6,7},{7,6},{8,9},{9,8},{10,11... | collective-permute-start | bytes 589832 | tf_op jit(solution)/shard_map/ppermute | solution.py:56
  70.7 1.5 collective-permute-start.17
  70.8 6.1 %copy-start.3 = (bf16[128,64]{1,0:T(8,128)(2,1)S(1)}, bf16[128,64]{1,0:T(8,128)(2,1)}, u32[]{:S(2)}) copy-start(bf16[128,64]{1,0:T(8,128)(2,1)} %copy.35.hi_ref) | copy-start | bytes 49156
  70.8 6.1 %copy-start.6 = (f32[128,64]{1,0:T(8,128)S(1)}, f32[128,64]{1,0:T(8,128)}, u32[]{:S(2)}) copy-start(f32[128,64]{1,0:T(8,128)} %copy.34) | copy-start | bytes 98308
  72.4 51.0 %collective-permute-start.19 = (bf16[1024,256]{1,0:T(8,128)(2,1)S(1)}, bf16[1024,256]{1,0:T(8,128)(2,1)S(1)}, u32[]{:S(2)}, u32[]{:S(2)}) collective-permute-start(bf16[1024,256]{1,0:T(8,128)(2,1)S(1)} %slice.154.kv_ref.refs_0_), channel_id=1, source_target_pairs={{0,64},{32,96},{64,128},{96,160},{128,192},{160,224},{192,0},{224,... | collective-permute-start | bytes 1572872 | tf_op jit(solution)/shard_map/ppermute | solution.py:60
  73.9 51.3 %collective-permute-start.20 = (bf16[1024,256]{1,0:T(8,128)(2,1)S(1)}, bf16[1024,256]{1,0:T(8,128)(2,1)S(1)}, u32[]{:S(2)}, u32[]{:S(2)}) collective-permute-start(bf16[1024,256]{1,0:T(8,128)(2,1)S(1)} %slice.154.kv_ref.refs_0_), channel_id=1, source_target_pairs={{0,192},{32,224},{64,0},{96,32},{128,64},{160,96},{192,128},{224,1... | collective-permute-start | bytes 1572872 | tf_op jit(solution)/shard_map/ppermute | solution.py:60
  74.5 31.8 %collective-permute-start.18 = (bf16[1024,128]{1,0:T(8,128)(2,1)S(1)}, bf16[1024,128]{1,0:T(8,128)(2,1)S(1)}, u32[]{:S(2)}, u32[]{:S(2)}) collective-permute-start(bf16[1024,128]{1,0:T(8,128)(2,1)S(1)} %slice.153.q_ref.qa_ref), channel_id=1, source_target_pairs={{0,32},{32,0},{64,96},{96,64},{128,160},{160,128},{192,224},{224,1... | collective-permute-start | bytes 786440 | tf_op jit(solution)/shard_map/ppermute | solution.py:64
  82.3 43.5 %copy-start.4 = (s32[8]{0:T(128)S(1)}, s32[8]{0:T(128)}, u32[]{:S(2)}) copy-start(s32[8]{0:T(128)} %order_ref.3) | copy-start | bytes 100
  123.4 10.4 %collective-permute-start.21 = (bf16[512,256]{1,0:T(8,128)(2,1)S(1)}, bf16[512,256]{1,0:T(8,128)(2,1)S(1)}, u32[]{:S(2)}, u32[]{:S(2)}) collective-permute-start(bf16[512,256]{1,0:T(8,128)(2,1)S(1)} %slice.155), channel_id=1, source_target_pairs={{0,64},{32,96},{64,128},{96,160},{128,192},{160,224},{192,0},{224,... | collective-permute-start | bytes 786440 | tf_op jit(solution)/shard_map/ppermute | solution.py:60
  125.2 8.6 %collective-permute-start.22 = (bf16[512,256]{1,0:T(8,128)(2,1)S(1)}, bf16[512,256]{1,0:T(8,128)(2,1)S(1)}, u32[]{:S(2)}, u32[]{:S(2)}) collective-permute-start(bf16[512,256]{1,0:T(8,128)(2,1)S(1)} %slice.156), channel_id=1, source_target_pairs={{0,192},{32,224},{64,0},{96,32},{128,64},{160,96},{192,128},{224,1... | collective-permute-start | bytes 786440 | tf_op jit(solution)/shard_map/ppermute | solution.py:60
  139.3 14.3 %all-to-all-start.1 = ((bf16[8,272,128]{2,1,0:T(8,128)(2,1)}), bf16[8,272,128]{2,1,0:T(8,128)(2,1)S(1)}, u32[]{:S(2)}, u32[]{:S(2)}) async-start(bf16[8,272,128]{2,1,0:T(8,128)(2,1)} %far_attention.1), calls=%async_computation.1 | async-start | bytes 1114112 | tf_op jit(solution)/shard_map/all_to_all | solution.py:469
  144.3 52.1 %reduce-scatter.2.cloned.1.call-start = ((), (), s32[]{:S(2)}) async-start(), calls=%async_computation.5 | async-start | bytes 1769472 | tf_op jit(solution)/shard_map/reduce_scatter | solution.py:474
  159.1 0.9 copy-start.5
  161.0 10.4 %all-to-all-start.2 = ((bf16[8,2,1024]{2,1,0:T(2,128)(2,1)}), bf16[8,2,1024]{2,1,0:T(2,128)(2,1)S(1)}, u32[]{:S(2)}, u32[]{:S(2)}) async-start(bf16[8,2,1024]{2,1,0:T(2,128)(2,1)} %reshape.58), calls=%async_computation.3 | async-start | bytes 65536 | tf_op jit(solution)/shard_map/all_to_all | solution.py:482
  172.5 13.3 %all-to-all-start.3 = ((bf16[32,2,1024]{2,1,0:T(2,128)(2,1)}), bf16[32,2,1024]{2,1,0:T(2,128)(2,1)S(1)}, u32[]{:S(2)}, u32[]{:S(2)}) async-start(bf16[32,2,1024]{2,1,0:T(2,128)(2,1)} %reshape.60), calls=%async_computation.4 | async-start | bytes 262144 | tf_op jit(solution)/shard_map/all_to_all | solution.py:486
  186.6 1.0 copy-start.7
  186.8 9.6 %copy-start.8 = (f32[1,3072]{1,0:T(1,128)S(1)}, f32[1,3072]{1,0:T(1,128)}, u32[]{:S(2)}) copy-start(f32[1,3072]{1,0:T(1,128)} %get-tuple-element.15) | copy-start | bytes 36868
Sparse Core Ops, SparseCore 0:
  159.3 37.0 reduce-scatter.1

commit v3 on v2

--- a/solution.py
+++ b/solution.py
@@ -82,11 +82,15 @@
 
 def norm_kernel(level_ref, hidden_ref, mod_ref, out_ref, gate_ref):
     values = hidden_ref[...].astype(jnp.float32)
+    row = pl.ds(level_ref[0] % MOD_ROWS, 1)
     center = values - jnp.mean(values, axis=-1, keepdims=True)
     spread = jnp.mean(center * center, axis=-1, keepdims=True)
     scaled = center * lax.rsqrt(spread + EPSILON)
-    out_ref[...] = (scaled * (1.0 + mod_ref[0, 1:2, :]) + mod_ref[0, 0:1, :]).astype(jnp.bfloat16)
-    gate_ref[...] = mod_ref[0, 2:3, :]
+    out_ref[...] = (scaled * (1.0 + mod_ref[1, row, :]) + mod_ref[0, row, :]).astype(jnp.bfloat16)
+    gate_ref[...] = mod_ref[2, row, :]
+
+
+MOD_ROWS = 8
 
 
 def normalize(levels, rows, modulation):
@@ -98,7 +102,7 @@
             grid=(1,),
             in_specs=[
                 pl.BlockSpec(rows.shape, lambda i, s: (0, 0)),
-                pl.BlockSpec((1, 3, width), lambda i, s: (s[0], 0, 0)),
+                pl.BlockSpec((3, MOD_ROWS, width), lambda i, s: (0, s[0] // MOD_ROWS, 0)),
             ],
             out_specs=[
                 pl.BlockSpec(rows.shape, lambda i, s: (0, 0)),
@@ -110,7 +114,28 @@
             jax.ShapeDtypeStruct((1, width), jnp.float32),
         ],
         name="normalize",
-    )(levels, rows, modulation)
+    )(levels, rows, modulation.transpose(1, 0, 2))
+
+
+def latent_kernel(w_ref, gate_ref, lw_ref, o_ref):
+    gated = w_ref[...].astype(jnp.float32) * gate_ref[...]
+    hi = gated.astype(jnp.bfloat16)
+    lo = (gated - hi.astype(jnp.float32)).astype(jnp.bfloat16)
+    out = dot_t(hi, lw_ref[...]) + dot_t(lo, lw_ref[...])
+    top = out.astype(jnp.bfloat16)
+    pv = out.shape[1]
+    o_ref[:, :pv] = top
+    o_ref[:, pv:] = (out - top.astype(jnp.float32)).astype(jnp.bfloat16)
+
+
+def latent_matrix(w, gate_row, latent_weight):
+    pv = latent_weight.shape[1]
+    return pl.pallas_call(
+        latent_kernel,
+        out_shape=jax.ShapeDtypeStruct((w.shape[0], 2 * pv), jnp.bfloat16),
+        compiler_params=pltpu.CompilerParams(vmem_limit_bytes=VMEM_LIMIT),
+        name="latent_matrix",
+    )(w, gate_row, latent_weight.T)
 
 
 def project_kernel(*refs):
@@ -150,8 +175,14 @@
 TILE = 128
 
 
-def self_kernel(s_ref, q_ref, kv_ref, hi_ref, lo_ref, o_ref, values):
+def used_slots(y, z):
+    return (y * NZ + z) * NC < HEADS
+
+
+def self_kernel(s_ref, q_ref, kv_ref, m_ref, o_ref, values):
     y, z, core = s_ref[1], s_ref[2], s_ref[3]
+    used = used_slots(y, z)
+    pv = o_ref.shape[2]
     values[:, :HD] = kv_ref[:, HD:]
     values[:, HD:] = jnp.ones((values.shape[0], HD), jnp.bfloat16)
     for t in range(q_ref.shape[0] // TILE):
@@ -159,10 +190,8 @@
         p = jnp.exp2(s - jnp.max(s, axis=1, keepdims=True)).astype(jnp.bfloat16)
         acc = jnp.dot(p, values[...], preferred_element_type=jnp.float32)
         att = (acc[:, :HD] / acc[:, HD:]).astype(jnp.bfloat16)
-        part = jnp.dot(att, hi_ref[...], preferred_element_type=jnp.float32) + jnp.dot(
-            att, lo_ref[...], preferred_element_type=jnp.float32
-        )
-        part = part.astype(jnp.bfloat16)
+        part = jnp.dot(att, m_ref[...], preferred_element_type=jnp.float32)
+        part = jnp.where(used, part[:, :pv] + part[:, pv:], 0.0).astype(jnp.bfloat16)
         for j in range(TILE // BLK):
             i = t * (TILE // BLK) + j
             d, quarter = i % NZ, i // NZ
@@ -170,15 +199,15 @@
             o_ref[at] = part[j * BLK : j * BLK + BLK]
 
 
-def self_attention(place, q, kv, hi, lo):
-    pv = hi.shape[1]
+def self_attention(place, q, kv, matrix):
+    pv = matrix.shape[1] // 2
     rows = q.shape[0]
     return pl.pallas_call(
         self_kernel,
         grid_spec=pltpu.PrefetchScalarGridSpec(
             num_scalar_prefetch=1,
             grid=(1,),
-            in_specs=[pl.BlockSpec(a.shape, lambda i, s: (0, 0)) for a in (q, kv, hi, lo)],
+            in_specs=[pl.BlockSpec(a.shape, lambda i, s: (0, 0)) for a in (q, kv, matrix)],
             out_specs=pl.BlockSpec((rows // BLK, BLK, pv), lambda i, s: (0, 0, 0)),
             scratch_shapes=[pltpu.VMEM((rows, 2 * HD), jnp.bfloat16)],
         ),
@@ -188,7 +217,7 @@
             flops=6 * rows * rows * HD, bytes_accessed=2**20, transcendentals=rows * rows
         ),
         name="self_attention",
-    )(place, q, kv, hi, lo)
+    )(place, q, kv, matrix)
 
 
 def visit(refs, q, keys, values, acc, top):
@@ -324,13 +353,14 @@
     )(order, place, qa, qb, acc, top, *blocks)
 
 
-def join_kernel(s_ref, in_ref, near_ref, far_ref, o_ref, a_ref):
+def join_kernel(s_ref, in_ref, w0_ref, w1_ref, w2_ref, w3_ref, o_ref, a_ref, w_ref):
     h, y, z, core = s_ref[0], s_ref[1], s_ref[2], s_ref[3]
     place = h * 4 + y * 2 + core
 
     @pl.when(pl.program_id(0) == 0)
     def _():
         for r in range(4):
+            used = used_slots(y ^ (r // 2), z)
             parts = []
             for dh in range(NH):
                 at = (dh * 4 + r) ^ place
@@ -342,7 +372,7 @@
             for half in range(2):
                 out = None
                 for (at, _), weight in zip(parts, e):
-                    w = (weight / norm)[half : half + 1, :]
+                    w = jnp.where(used, weight / norm, 0.0)[half : half + 1, :]
                     col = jnp.broadcast_to(w, (128, 128)).T
                     term = in_ref[at, half * 128 : half * 128 + 128, :].astype(jnp.float32) * col
                     out = term if out is None else out + term
@@ -351,29 +381,32 @@
                     start = pl.multiple_of(((z + half * 4 + j) % NZ) * BLK, BLK)
                     a_ref[pl.ds(start, BLK), r * HD : r * HD + HD] = out[j * BLK : j * BLK + BLK]
 
-    o_ref[...] = (
-        jnp.dot(a_ref[:, : 2 * HD], near_ref[...], preferred_element_type=jnp.float32)
-        + jnp.dot(a_ref[:, 2 * HD :], far_ref[...], preferred_element_type=jnp.float32)
-    ).astype(jnp.bfloat16)
-
-
-def join_heads(place, received, near, far):
-    width = near.shape[1]
+    for r, ref in enumerate((w0_ref, w1_ref, w2_ref, w3_ref)):
+        w_ref[r * HD : r * HD + HD, :] = ref[...]
+    o_ref[...] = jnp.dot(a_ref[...], w_ref[...], preferred_element_type=jnp.float32).astype(
+        jnp.bfloat16
+    )
+
+
+def join_heads(place, received, weights):
+    width = weights[0].shape[1]
     step = width // 4
-    cut = pl.BlockSpec((2 * HD, step), lambda i, s: (0, i))
     return pl.pallas_call(
         join_kernel,
         grid_spec=pltpu.PrefetchScalarGridSpec(
             num_scalar_prefetch=1,
             grid=(4,),
-            in_specs=[whole(received), cut, cut],
+            in_specs=[whole(received)] + [pl.BlockSpec((HD, step), lambda i, s: (0, i))] * 4,
             out_specs=pl.BlockSpec((QUARTER, step), lambda i, s: (0, i)),
-            scratch_shapes=[pltpu.VMEM((QUARTER, 4 * HD), jnp.bfloat16)],
+            scratch_shapes=[
+                pltpu.VMEM((QUARTER, 4 * HD), jnp.bfloat16),
+                pltpu.VMEM((4 * HD, step), jnp.bfloat16),
+            ],
         ),
         out_shape=jax.ShapeDtypeStruct((QUARTER, width), jnp.bfloat16),
         compiler_params=pltpu.CompilerParams(vmem_limit_bytes=VMEM_LIMIT),
         name="join_heads",
-    )(place, received, near, far)
+    )(place, received, *weights)
 
 
 def decode(latents, root_kernel):
@@ -426,17 +459,6 @@
     w_own = in_weight[0]
     own_blocks, other_blocks = gather_class(normed)
     w_oth = move_core(w_own)
-    out_w = jnp.where(seq_me < HEADS, out_weight[0], jnp.zeros_like(out_weight[0]))
-    pair = jnp.concatenate([out_w, move_core(out_w)], axis=0)
-    head_latent = jnp.dot(
-        out_w.astype(jnp.float32) * gate_row,
-        latent_weight.astype(jnp.float32),
-        precision=lax.Precision.HIGH,
-    )
-    latent_hi = head_latent.astype(jnp.bfloat16)
-    latent_lo = (head_latent - latent_hi.astype(jnp.float32)).astype(jnp.bfloat16)
-    own_latents = jnp.dot(hidden[0], latent_weight, preferred_element_type=jnp.float32)
-
     mine_a, theirs_a = project(own_blocks, w_own, w_oth)
     mine_b, theirs_b = project(other_blocks, w_own, w_oth)
     triples = jnp.concatenate([mine_a, move_core(theirs_a), mine_b, move_core(theirs_b)], axis=0)
@@ -448,13 +470,15 @@
     q_hi = move_hi(q)
     kv_far = (move_x(kv_up[:half], 1), move_x(kv_dn[half:], -1))
 
-    far_pair = move_y(lax.optimization_barrier((pair, other_blocks[4]))[0])
-
-    part = self_attention(place, q, kv, latent_hi, latent_lo)
+    out_w, q = lax.optimization_barrier((out_weight[0], q))
+    part = self_attention(place, q, kv, latent_matrix(out_w, gate_row, latent_weight))
     q_hi, part = lax.optimization_barrier((q_hi, part))
+
+    out_w, q_hi = lax.optimization_barrier((out_w, q_hi))
+    w_core, w_far = move_core(out_w), move_y(out_w)
+    weights = (out_w, w_core, w_far, move_core(w_far))
+
     acc, top = near_attention(span_order, place, q, q_hi, ((kv,), (kv_up,), (kv_dn,)))
-    part = lax.all_to_all(part, "seq", 0, 0, tiled=True)
-    acc, part = lax.optimization_barrier((acc, part))
     chunks = far_attention(span_order, place, q, q_hi, acc, top, kv_far)
     groups = [
         [
@@ -469,13 +493,15 @@
     received = lax.all_to_all(
         chunks, ("span", "seq"), 0, 0, tiled=True, axis_index_groups=groups
     )
-    partial = join_heads(place, received, pair, far_pair)
+    partial = join_heads(place, received, weights)
     z_groups = [[seq_at(yy, j, cc) for j in range(NZ)] for yy in range(NY) for cc in range(NC)]
     summed = lax.psum_scatter(
         partial, "seq", scatter_dimension=0, tiled=True, axis_index_groups=z_groups
     ).astype(jnp.float32)
     block_out = (hidden[0].astype(jnp.float32) + gate_row * summed).astype(jnp.bfloat16)[None]
 
+    part = lax.all_to_all(part, "seq", 0, 0, tiled=True)
+    own_latents = jnp.dot(hidden[0], latent_weight, preferred_element_type=jnp.float32)
     latents = (jnp.sum(part.astype(jnp.float32), axis=0) + own_latents).astype(jnp.bfloat16)
     group_ids = jnp.arange(span_order.shape[0], dtype=jnp.int32)
     root = jnp.sum(jnp.where(span_order == 0, group_ids, 0))

time: 207 us -> 183 us (0.88)
  waiting for transfers between devices: 77.3 us -> 60.8 us
  starting transfers between devices: 41.5 us -> 50.9 us
  Pallas kernels: 32.2 us -> 24.5 us
  other arithmetic: 7.48 us -> 2.75 us
  matrix products: 3.44 us -> 1.02 us
    ppermute x1, waiting for transfers between devices: 24 us -> 1.52 us  [move_hi(): return lax.ppermute(a, 'span', span_route(dh=1))]
    all_to_all x1, starting transfers between devices: 4.17 us -> 15.5 us  [per_device(): lax.all_to_all(jnp.broadcast_to(latents[None], (NX * NH, BLK, pv)), 'span...]
    ppermute x4, waiting for transfers between devices: 0.01 us -> 10.9 us  [move_x(): return lax.ppermute(a, 'span', span_route(dx=d))]
    ppermute x7, waiting for transfers between devices: 3.68 us -> 13.4 us  [move_y(): return lax.ppermute(a, 'seq', seq_route(dy=1))]
    reduce_scatter x1, waiting for transfers between devices: 7.99 us -> 0.01 us  [per_device(): lax.psum_scatter(partial, 'seq', scatter_dimension=0, tiled=True, axis_in...]
    ppermute x9, waiting for transfers between devices: 18.5 us -> 11.8 us  [move_z(): return lax.ppermute(a, 'seq', seq_route(dz=d))]
    pallas_call x1, Pallas kernels: 5.5 us -> 1.37 us  [far_attention(): pl.pallas_call(far_kernel, grid_spec=pltpu.PrefetchScalarGridSpec(num_sca...]
    concatenate x1 -> x0, other arithmetic: 2.64 us -> none  [per_device(): pair = jnp.concatenate([out_w, move_core(out_w)], axis=0)]
  transfers between devices with their start and end apart: 29 -> 30, of which waited for: 14 -> 14; matrix products, arithmetic and copies ran while one was open for 9% -> 4% of each run, Pallas kernels for 13% -> 11%
where the time goes in v3:
time: 183 us; the launch traced here: 181 us
  waiting for transfers between devices  60.8 us (33%)
  starting transfers between devices  50.9 us (28%)
  Pallas kernels  24.5 us (13%)
  between operations  17.1 us (9%)
  blocking collectives  15.7 us (9%)
  local copies, waits for them, and re-layouts  8.22 us (4%)
  other arithmetic  2.75 us (2%)
    all_to_all x1, blocking collectives, per_device(): part = lax.all_to_all(part, 'seq', 0, 0, tiled=True)  15.7 us
    all_to_all x1, starting transfers between devices, per_device(): lax.all_to_all(jnp.broadcast_to(latents[None], (NX * NH, BLK, pv)), 'span...  15.5 us
    ppermute x9, starting transfers between devices, move_z(): return lax.ppermute(a, 'seq', seq_route(dz=d))  14.4 us
    ppermute x7, waiting for transfers between devices, move_y(): return lax.ppermute(a, 'seq', seq_route(dy=1))  13.4 us
    ppermute x9, waiting for transfers between devices, move_z(): return lax.ppermute(a, 'seq', seq_route(dz=d))  11.8 us
    ppermute x4, waiting for transfers between devices, move_x(): return lax.ppermute(a, 'span', span_route(dx=d))  10.9 us
    all_to_all x1, waiting for transfers between devices, per_device(): lax.all_to_all(chunks, ('span', 'seq'), 0, 0, tiled=True, axis_index_grou...  9.26 us
    all_to_all x1, waiting for transfers between devices, per_device(): lax.all_to_all(jnp.broadcast_to(latents, (seq_count, BLK, pv)), 'seq', 0,...  8.94 us
  transfers between devices with their start and end apart: 30, of which 14 were waited for; matrix products, arithmetic and copies ran while one was open for 4% of the time, Pallas kernels for 11%

profile of v3, /device:TPU:10, one launch (start us, length us, event | category | flops | bytes accessed | tf_op | source)
XLA Modules:
  0.0 181.1 jit_solution(5087587973368675055)
XLA Ops:
  7.2 0.1 collective-permute-start.7
  7.9 2.0 %normalize.1 = (bf16[32,3072]{1,0:T(8,128)(2,1)}, f32[1,3072]{1,0:T(1,128)}) custom-call(s32[1]{0:T(128)S(6)} %copy.28.level_ref, bf16[32,3072]{1,0:T(8,128)(2,1)} %bitcast.48, f32[3,16,3072]{2,1,0:T(8,128)} %bitcast.49), custom_call_target="tpu_custom_call" | custom-call | tf_op jit(solution)/shard_map/normalize/pallas_call | solution.py:98
  10.0 1.9 %collective-permute-start.3 = (bf16[32,3072]{1,0:T(8,128)(2,1)}, bf16[32,3072]{1,0:T(8,128)(2,1)S(1)}, u32[]{:S(2)}, u32[]{:S(2)}) collective-permute-start(bf16[32,3072]{1,0:T(8,128)(2,1)} %get-tuple-element.17.refs_0_), channel_id=1, source_target_pairs={{0,2},{1,3},{2,4},{3,5},{4,6},{5,7},{6,8},{7,9},{8,10},{9,11},{10,... | collective-permute-start | bytes 589832 | tf_op jit(solution)/shard_map/ppermute | solution.py:48
  11.9 3.9 %collective-permute-start = (bf16[32,3072]{1,0:T(8,128)(2,1)}, bf16[32,3072]{1,0:T(8,128)(2,1)S(1)}, u32[]{:S(2)}, u32[]{:S(2)}) collective-permute-start(bf16[32,3072]{1,0:T(8,128)(2,1)} %get-tuple-element.17.refs_0_), channel_id=1, source_target_pairs={{0,14},{1,15},{2,0},{3,1},{4,2},{5,3},{6,4},{7,5},{8,6},{9,7},{10,... | collective-permute-start | bytes 589832 | tf_op jit(solution)/shard_map/ppermute | solution.py:48
  15.8 5.8 %collective-permute-done.3.refs_7_ = bf16[32,3072]{1,0:T(8,128)(2,1)S(1)} collective-permute-done((bf16[32,3072]{1,0:T(8,128)(2,1)}, bf16[32,3072]{1,0:T(8,128)(2,1)S(1)}, u32[]{:S(2)}, u32[]{:S(2)}) %collective-permute-start.3) | collective-permute-done | bytes 196640 | tf_op jit(solution)/shard_map/ppermute | solution.py:48
  21.6 3.2 %collective-permute-start.1 = (bf16[32,3072]{1,0:T(8,128)(2,1)S(1)}, bf16[32,3072]{1,0:T(8,128)(2,1)S(1)}, u32[]{:S(2)}, u32[]{:S(2)}) collective-permute-start(bf16[32,3072]{1,0:T(8,128)(2,1)S(1)} %collective-permute-done.refs_1_), channel_id=1, source_target_pairs={{0,14},{1,15},{2,0},{3,1},{4,2},{5,3},{6,4},{7,5},{8,6},{9,7},{10,... | collective-permute-start | bytes 589832 | tf_op jit(solution)/shard_map/ppermute | solution.py:48
  24.8 0.4 collective-permute-start.9
  25.3 4.2 %collective-permute-done.4.refs_6_ = bf16[32,3072]{1,0:T(8,128)(2,1)S(1)} collective-permute-done((bf16[32,3072]{1,0:T(8,128)(2,1)S(1)}, bf16[32,3072]{1,0:T(8,128)(2,1)S(1)}, u32[]{:S(2)}, u32[]{:S(2)}) %collective-permute-start.4) | collective-permute-done | bytes 196640 | tf_op jit(solution)/shard_map/ppermute | solution.py:48
  29.6 3.2 %collective-permute-start.2 = (bf16[32,3072]{1,0:T(8,128)(2,1)S(1)}, bf16[32,3072]{1,0:T(8,128)(2,1)S(1)}, u32[]{:S(2)}, u32[]{:S(2)}) collective-permute-start(bf16[32,3072]{1,0:T(8,128)(2,1)S(1)} %collective-permute-done.1.refs_2_), channel_id=1, source_target_pairs={{0,14},{1,15},{2,0},{3,1},{4,2},{5,3},{6,4},{7,5},{8,6},{9,7},{10,... | collective-permute-start | bytes 589832 | tf_op jit(solution)/shard_map/ppermute | solution.py:48
  32.8 0.4 collective-permute-start.11
  33.2 1.6 collective-permute-start.14
  34.8 1.8 collective-permute-done.5.refs_5_
  36.6 0.5 collective-permute-start.10
  37.1 3.5 %collective-permute-done.11.refs_2_ = bf16[32,3072]{1,0:T(8,128)(2,1)S(1)} collective-permute-done((bf16[32,3072]{1,0:T(8,128)(2,1)S(1)}, bf16[32,3072]{1,0:T(8,128)(2,1)S(1)}, u32[]{:S(2)}, u32[]{:S(2)}) %collective-permute-start.11) | collective-permute-done | bytes 196640 | tf_op jit(solution)/shard_map/ppermute | solution.py:52
  40.6 0.4 collective-permute-start.16
  41.1 3.8 %collective-permute-done.14.refs_6_ = bf16[32,3072]{1,0:T(8,128)(2,1)S(1)} collective-permute-done((bf16[32,3072]{1,0:T(8,128)(2,1)S(1)}, bf16[32,3072]{1,0:T(8,128)(2,1)S(1)}, u32[]{:S(2)}, u32[]{:S(2)}) %collective-permute-start.14) | collective-permute-done | bytes 196640 | tf_op jit(solution)/shard_map/ppermute | solution.py:52
  44.8 2.0 %collective-permute-start.15 = (bf16[32,3072]{1,0:T(8,128)(2,1)S(1)}, bf16[32,3072]{1,0:T(8,128)(2,1)S(1)}, u32[]{:S(2)}, u32[]{:S(2)}) collective-permute-start(bf16[32,3072]{1,0:T(8,128)(2,1)S(1)} %collective-permute-done.14.refs_6_), channel_id=1, source_target_pairs={{0,2},{1,3},{2,4},{3,5},{4,6},{5,7},{6,8},{7,9},{8,10},{9,11},{10,... | collective-permute-start | bytes 589832 | tf_op jit(solution)/shard_map/ppermute | solution.py:48
  46.9 0.5 collective-permute-start.13
  47.3 1.7 copy-done.1
  49.0 0.9 copy-done.7
  49.9 1.8 %project.2 = (bf16[256,384]{1,0:T(8,128)(2,1)S(1)}, bf16[256,384]{1,0:T(8,128)(2,1)S(1)}) custom-call(bf16[32,3072]{1,0:T(8,128)(2,1)S(1)} %copy-done.7, bf16[32,3072]{1,0:T(8,128)(2,1)S(1)} %collective-permute-done.refs_1_, bf16[32,3072]{1,0:T(8,128)(2,1)S(1)} %collective-permute-done.1.refs_2_, bf16[32,3072]{1,0:T(8,128)(2,1)S(1)} %collective-permute-done.2.refs_3_, ...), custom_call_target="tpu_custom_call" | custom-call | flops 1207959552 | bytes 6291456 | tf_op jit(solution)/shard_map/project/pallas_call | solution.py:155
  51.7 0.1 collective-permute-start.8
  51.8 1.0 collective-permute-done.16.refs_7_
  52.8 2.1 %collective-permute-done.13.refs_4_ = bf16[32,3072]{1,0:T(8,128)(2,1)S(1)} collective-permute-done((bf16[32,3072]{1,0:T(8,128)(2,1)S(1)}, bf16[32,3072]{1,0:T(8,128)(2,1)S(1)}, u32[]{:S(2)}, u32[]{:S(2)}) %collective-permute-start.13) | collective-permute-done | bytes 196640 | tf_op jit(solution)/shard_map/ppermute | solution.py:52
  55.0 1.8 %project.3 = (bf16[256,384]{1,0:T(8,128)(2,1)S(1)}, bf16[256,384]{1,0:T(8,128)(2,1)S(1)}) custom-call(bf16[32,3072]{1,0:T(8,128)(2,1)S(1)} %collective-permute-done.9.refs_0_, bf16[32,3072]{1,0:T(8,128)(2,1)S(1)} %collective-permute-done.10.refs_1_, bf16[32,3072]{1,0:T(8,128)(2,1)S(1)} %collective-permute-done.11.refs_2_, ...), custom_call_target="tpu_custom_call" | custom-call | flops 1207959552 | bytes 6291456 | tf_op jit(solution)/shard_map/project/pallas_call | solution.py:155
  57.0 1.3 collective-permute-done.17
  58.4 2.4 %collective-permute-start.18 = (bf16[1024,128]{1,0:T(8,128)(2,1)S(1)}, bf16[1024,128]{1,0:T(8,128)(2,1)S(1)}, u32[]{:S(2)}, u32[]{:S(2)}) collective-permute-start(bf16[1024,128]{1,0:T(8,128)(2,1)S(1)} %slice.153.q_ref.qa_ref), channel_id=1, source_target_pairs={{0,32},{32,0},{64,96},{96,64},{128,160},{160,128},{192,224},{224,1... | collective-permute-start | bytes 786440 | tf_op jit(solution)/shard_map/ppermute | solution.py:64
  60.9 0.6 latent_matrix.1.m_ref
  61.6 5.2 %self_attention.1 = bf16[32,32,64]{2,1,0:T(8,128)(2,1)S(1)} custom-call(s32[5]{0:T(128)S(1)} %stack.23.s_ref, bf16[1024,128]{1,0:T(8,128)(2,1)S(1)} %slice.153.q_ref.qa_ref, bf16[1024,256]{1,0:T(8,128)(2,1)S(1)} %slice.154.kv_ref.refs_0_, bf16[128,128]{1,0:T(8,128)(2,1)S(1)} %latent_matrix.1.m_ref), custom_call_target="tpu_custom_call" | custom-call | flops 805306368 | bytes 1048576 | tf_op jit(solution)/shard_map/self_attention/pallas_call | solution.py:205
  66.8 1.5 collective-permute-done.18.qb_ref
  68.3 0.5 collective-permute-start.24
  68.8 1.5 collective-permute-start.19
  70.3 0.5 collective-permute-start.20
  70.8 10.8 %collective-permute-done.19.refs_1_ = bf16[1024,256]{1,0:T(8,128)(2,1)S(1)} collective-permute-done((bf16[1024,256]{1,0:T(8,128)(2,1)S(1)}, bf16[1024,256]{1,0:T(8,128)(2,1)S(1)}, u32[]{:S(2)}, u32[]{:S(2)}) %collective-permute-start.19) | collective-permute-done | bytes 524320 | tf_op jit(solution)/shard_map/ppermute | solution.py:60
  81.7 1.6 collective-permute-start.21
  83.3 0.8 collective-permute-start.22
  84.1 3.0 %collective-permute-done.24.w2_ref = bf16[128,3072]{1,0:T(8,128)(2,1)S(1)} collective-permute-done((bf16[128,3072]{1,0:T(8,128)(2,1)S(1)}, bf16[128,3072]{1,0:T(8,128)(2,1)S(1)}, u32[]{:S(2)}, u32[]{:S(2)}) %collective-permute-start.24) | collective-permute-done | bytes 786464 | tf_op jit(solution)/shard_map/ppermute | solution.py:52
  87.1 6.5 %near_attention.1 = (f32[2,1024,256]{2,1,0:T(8,128)S(1)}, f32[2,1024,128]{2,1,0:T(8,128)S(1)}) custom-call(s32[8]{0:T(128)S(1)} %copy-done.9, s32[5]{0:T(128)S(1)} %stack.23.s_ref, bf16[1024,128]{1,0:T(8,128)(2,1)S(1)} %slice.153.q_ref.qa_ref, bf16[1024,128]{1,0:T(8,128)(2,1)S(1)} %collective-permute-done.18.qb_ref, ...), custom_call_target="tpu_custom_call" | custom-call | flops 4831838208 | bytes 4194304 | tf_op jit(solution)/shard_map/near_attention/pallas_call | solution.py:307
  93.6 1.4 far_attention.1
  95.0 0.8 copy-done.5
  95.8 3.9 %all-to-all-start = ((bf16[8,272,128]{2,1,0:T(8,128)(2,1)}), bf16[8,272,128]{2,1,0:T(8,128)(2,1)S(1)}, u32[]{:S(2)}, u32[]{:S(2)}) async-start(bf16[8,272,128]{2,1,0:T(8,128)(2,1)} %copy-done.5), calls=%async_computation | async-start | bytes 1114112 | tf_op jit(solution)/shard_map/all_to_all | solution.py:493
  99.7 9.3 %all-to-all-done.in_ref = bf16[8,272,128]{2,1,0:T(8,128)(2,1)S(1)} async-done(((bf16[8,272,128]{2,1,0:T(8,128)(2,1)}), bf16[8,272,128]{2,1,0:T(8,128)(2,1)S(1)}, u32[]{:S(2)}, u32[]{:S(2)}) %all-to-all-start) | async-done | bytes 557088 | tf_op jit(solution)/shard_map/all_to_all | solution.py:493
  109.0 5.2 %join_heads.1 = bf16[256,3072]{1,0:T(8,128)(2,1)} custom-call(s32[5]{0:T(128)S(1)} %stack.23.s_ref, bf16[8,272,128]{2,1,0:T(8,128)(2,1)S(1)} %all-to-all-done.in_ref, bf16[128,3072]{1,0:T(8,128)(2,1)S(1)} %bitcast.45, bf16[128,3072]{1,0:T(8,128)(2,1)S(1)} %collective-permute-done.23.w1_ref, bf16[128,3072]{1,0:T(8,128)(2,1)S(1)} %collective-permute-done.24.w2_ref, ...), custom_call_target="tpu_custom_call" | custom-call | tf_op jit(solution)/shard_map/join_heads/pallas_call | solution.py:394
  114.2 1.2 reshape.53
  115.4 15.7 %all_to_all.20 = bf16[32,2,1024]{2,1,0:T(2,128)(2,1)S(1)} all-to-all(bf16[32,2,1024]{2,1,0:T(2,128)(2,1)S(1)} %reshape.53), channel_id=1, replica_groups=mesh['span'=8,'seq'=32] {'seq'}, dimensions={0} | all-to-all | bytes 262144 | tf_op jit(solution)/shard_map/all_to_all | solution.py:503
  131.0 0.2 reshape.54
  131.4 0.2 fusion.1
  131.6 0.7 reshape.55
  132.3 15.5 %all-to-all-start.2 = ((bf16[8,2,1024]{2,1,0:T(2,128)(2,1)}), bf16[8,2,1024]{2,1,0:T(2,128)(2,1)S(1)}, u32[]{:S(2)}, u32[]{:S(2)}) async-start(bf16[8,2,1024]{2,1,0:T(2,128)(2,1)} %reshape.55), calls=%async_computation.3 | async-start | bytes 65536 | tf_op jit(solution)/shard_map/all_to_all | solution.py:508
  147.8 0.6 fusion.3
  150.4 3.7 %all-to-all-done.2 = bf16[8,2,1024]{2,1,0:T(2,128)(2,1)S(1)} async-done(((bf16[8,2,1024]{2,1,0:T(2,128)(2,1)}), bf16[8,2,1024]{2,1,0:T(2,128)(2,1)S(1)}, u32[]{:S(2)}, u32[]{:S(2)}) %all-to-all-start.2) | async-done | bytes 32800 | tf_op jit(solution)/shard_map/all_to_all | solution.py:508
  154.1 0.1 reshape.56
  154.3 0.8 reshape.57
  155.1 5.8 %all-to-all-start.3 = ((bf16[32,2,1024]{2,1,0:T(2,128)(2,1)}), bf16[32,2,1024]{2,1,0:T(2,128)(2,1)S(1)}, u32[]{:S(2)}, u32[]{:S(2)}) async-start(bf16[32,2,1024]{2,1,0:T(2,128)(2,1)} %reshape.57), calls=%async_computation.4 | async-start | bytes 262144 | tf_op jit(solution)/shard_map/all_to_all | solution.py:512
  161.0 8.9 %all-to-all-done.3 = bf16[32,2,1024]{2,1,0:T(2,128)(2,1)S(1)} async-done(((bf16[32,2,1024]{2,1,0:T(2,128)(2,1)}), bf16[32,2,1024]{2,1,0:T(2,128)(2,1)S(1)}, u32[]{:S(2)}, u32[]{:S(2)}) %all-to-all-start.3) | async-done | bytes 131104 | tf_op jit(solution)/shard_map/all_to_all | solution.py:512
  169.9 0.2 reshape.58
  170.2 0.3 copy.16
  170.5 0.1 pad_maximum_fusion
  170.6 0.1 copy.21
  170.7 0.1 copy.20
  170.9 0.1 copy.19
  171.4 0.3 concatenate.11
  171.7 0.8 fusion
  172.5 1.7 fusion.2
  (67 shorter events, 1.1 us)
Async XLA Ops:
  7.2 164.6 %copy-start = (bf16[3,3,3,16,64]{4,3,2,1,0:T(8,128)(2,1)S(1)}, bf16[3,3,3,16,64]{4,3,2,1,0:T(8,128)(2,1)}, u32[]{:S(2)}) copy-start(bf16[3,3,3,16,64]{4,3,2,1,0:T(8,128)(2,1)} %param.15) | copy-start | bytes 165892
  7.2 39.7 %collective-permute-start.7 = (bf16[3072,384]{1,0:T(8,128)(2,1)}, bf16[3072,384]{1,0:T(8,128)(2,1)S(1)}, u32[]{:S(2)}, u32[]{:S(2)}) collective-permute-start(bf16[3072,384]{1,0:T(8,128)(2,1)} %bitcast.39), channel_id=1, source_target_pairs={{0,1},{1,0},{2,3},{3,2},{4,5},{5,4},{6,7},{7,6},{8,9},{9,8},{10,11... | collective-permute-start | bytes 7077896 | tf_op jit(solution)/shard_map/ppermute | solution.py:56
  10.0 11.6 %collective-permute-start.3 = (bf16[32,3072]{1,0:T(8,128)(2,1)}, bf16[32,3072]{1,0:T(8,128)(2,1)S(1)}, u32[]{:S(2)}, u32[]{:S(2)}) collective-permute-start(bf16[32,3072]{1,0:T(8,128)(2,1)} %get-tuple-element.17.refs_0_), channel_id=1, source_target_pairs={{0,2},{1,3},{2,4},{3,5},{4,6},{5,7},{6,8},{7,9},{8,10},{9,11},{10,... | collective-permute-start | bytes 589832 | tf_op jit(solution)/shard_map/ppermute | solution.py:48
  11.9 9.7 %collective-permute-start = (bf16[32,3072]{1,0:T(8,128)(2,1)}, bf16[32,3072]{1,0:T(8,128)(2,1)S(1)}, u32[]{:S(2)}, u32[]{:S(2)}) collective-permute-start(bf16[32,3072]{1,0:T(8,128)(2,1)} %get-tuple-element.17.refs_0_), channel_id=1, source_target_pairs={{0,14},{1,15},{2,0},{3,1},{4,2},{5,3},{6,4},{7,5},{8,6},{9,7},{10,... | collective-permute-start | bytes 589832 | tf_op jit(solution)/shard_map/ppermute | solution.py:48
  21.6 7.9 %collective-permute-start.4 = (bf16[32,3072]{1,0:T(8,128)(2,1)S(1)}, bf16[32,3072]{1,0:T(8,128)(2,1)S(1)}, u32[]{:S(2)}, u32[]{:S(2)}) collective-permute-start(bf16[32,3072]{1,0:T(8,128)(2,1)S(1)} %collective-permute-done.3.refs_7_), channel_id=1, source_target_pairs={{0,2},{1,3},{2,4},{3,5},{4,6},{5,7},{6,8},{7,9},{8,10},{9,11},{10,... | collective-permute-start | bytes 589832 | tf_op jit(solution)/shard_map/ppermute | solution.py:48
  21.6 7.9 %collective-permute-start.1 = (bf16[32,3072]{1,0:T(8,128)(2,1)S(1)}, bf16[32,3072]{1,0:T(8,128)(2,1)S(1)}, u32[]{:S(2)}, u32[]{:S(2)}) collective-permute-start(bf16[32,3072]{1,0:T(8,128)(2,1)S(1)} %collective-permute-done.refs_1_), channel_id=1, source_target_pairs={{0,14},{1,15},{2,0},{3,1},{4,2},{5,3},{6,4},{7,5},{8,6},{9,7},{10,... | collective-permute-start | bytes 589832 | tf_op jit(solution)/shard_map/ppermute | solution.py:48
  24.8 8.4 %collective-permute-start.9 = (bf16[32,3072]{1,0:T(8,128)(2,1)}, bf16[32,3072]{1,0:T(8,128)(2,1)S(1)}, u32[]{:S(2)}, u32[]{:S(2)}) collective-permute-start(bf16[32,3072]{1,0:T(8,128)(2,1)} %get-tuple-element.17.refs_0_), channel_id=1, source_target_pairs={{0,16},{1,17},{2,18},{3,19},{4,20},{5,21},{6,22},{7,23},{8,24},{9,... | collective-permute-start | bytes 589832 | tf_op jit(solution)/shard_map/ppermute | solution.py:52
  29.5 7.1 %collective-permute-start.5 = (bf16[32,3072]{1,0:T(8,128)(2,1)S(1)}, bf16[32,3072]{1,0:T(8,128)(2,1)S(1)}, u32[]{:S(2)}, u32[]{:S(2)}) collective-permute-start(bf16[32,3072]{1,0:T(8,128)(2,1)S(1)} %collective-permute-done.4.refs_6_), channel_id=1, source_target_pairs={{0,2},{1,3},{2,4},{3,5},{4,6},{5,7},{6,8},{7,9},{8,10},{9,11},{10,... | collective-permute-start | bytes 589832 | tf_op jit(solution)/shard_map/ppermute | solution.py:48
  29.6 7.1 %collective-permute-start.2 = (bf16[32,3072]{1,0:T(8,128)(2,1)S(1)}, bf16[32,3072]{1,0:T(8,128)(2,1)S(1)}, u32[]{:S(2)}, u32[]{:S(2)}) collective-permute-start(bf16[32,3072]{1,0:T(8,128)(2,1)S(1)} %collective-permute-done.1.refs_2_), channel_id=1, source_target_pairs={{0,14},{1,15},{2,0},{3,1},{4,2},{5,3},{6,4},{7,5},{8,6},{9,7},{10,... | collective-permute-start | bytes 589832 | tf_op jit(solution)/shard_map/ppermute | solution.py:48
  32.8 7.8 %collective-permute-start.11 = (bf16[32,3072]{1,0:T(8,128)(2,1)S(1)}, bf16[32,3072]{1,0:T(8,128)(2,1)S(1)}, u32[]{:S(2)}, u32[]{:S(2)}) collective-permute-start(bf16[32,3072]{1,0:T(8,128)(2,1)S(1)} %collective-permute-done.1.refs_2_), channel_id=1, source_target_pairs={{0,16},{1,17},{2,18},{3,19},{4,20},{5,21},{6,22},{7,23},{8,24},{9,... | collective-permute-start | bytes 589832 | tf_op jit(solution)/shard_map/ppermute | solution.py:52
  33.2 11.6 %collective-permute-start.14 = (bf16[32,3072]{1,0:T(8,128)(2,1)S(1)}, bf16[32,3072]{1,0:T(8,128)(2,1)S(1)}, u32[]{:S(2)}, u32[]{:S(2)}) collective-permute-start(bf16[32,3072]{1,0:T(8,128)(2,1)S(1)} %collective-permute-done.4.refs_6_), channel_id=1, source_target_pairs={{0,16},{1,17},{2,18},{3,19},{4,20},{5,21},{6,22},{7,23},{8,24},{9,... | collective-permute-start | bytes 589832 | tf_op jit(solution)/shard_map/ppermute | solution.py:52
  36.6 8.2 %collective-permute-start.6 = (bf16[32,3072]{1,0:T(8,128)(2,1)S(1)}, bf16[32,3072]{1,0:T(8,128)(2,1)S(1)}, u32[]{:S(2)}, u32[]{:S(2)}) collective-permute-start(bf16[32,3072]{1,0:T(8,128)(2,1)S(1)} %collective-permute-done.5.refs_5_), channel_id=1, source_target_pairs={{0,2},{1,3},{2,4},{3,5},{4,6},{5,7},{6,8},{7,9},{8,10},{9,11},{10,... | collective-permute-start | bytes 589832 | tf_op jit(solution)/shard_map/ppermute | solution.py:48
  36.6 15.1 %collective-permute-start.10 = (bf16[32,3072]{1,0:T(8,128)(2,1)S(1)}, bf16[32,3072]{1,0:T(8,128)(2,1)S(1)}, u32[]{:S(2)}, u32[]{:S(2)}) collective-permute-start(bf16[32,3072]{1,0:T(8,128)(2,1)S(1)} %collective-permute-done.refs_1_), channel_id=1, source_target_pairs={{0,16},{1,17},{2,18},{3,19},{4,20},{5,21},{6,22},{7,23},{8,24},{9,... | collective-permute-start | bytes 589832 | tf_op jit(solution)/shard_map/ppermute | solution.py:52
  40.6 12.2 %collective-permute-start.16 = (bf16[32,3072]{1,0:T(8,128)(2,1)S(1)}, bf16[32,3072]{1,0:T(8,128)(2,1)S(1)}, u32[]{:S(2)}, u32[]{:S(2)}) collective-permute-start(bf16[32,3072]{1,0:T(8,128)(2,1)S(1)} %collective-permute-done.3.refs_7_), channel_id=1, source_target_pairs={{0,16},{1,17},{2,18},{3,19},{4,20},{5,21},{6,22},{7,23},{8,24},{9,... | collective-permute-start | bytes 589832 | tf_op jit(solution)/shard_map/ppermute | solution.py:52
  44.8 8.0 %collective-permute-start.12 = (bf16[32,3072]{1,0:T(8,128)(2,1)S(1)}, bf16[32,3072]{1,0:T(8,128)(2,1)S(1)}, u32[]{:S(2)}, u32[]{:S(2)}) collective-permute-start(bf16[32,3072]{1,0:T(8,128)(2,1)S(1)} %collective-permute-done.11.refs_2_), channel_id=1, source_target_pairs={{0,14},{1,15},{2,0},{3,1},{4,2},{5,3},{6,4},{7,5},{8,6},{9,7},{10,... | collective-permute-start | bytes 589832 | tf_op jit(solution)/shard_map/ppermute | solution.py:48
  44.8 8.0 %collective-permute-start.15 = (bf16[32,3072]{1,0:T(8,128)(2,1)S(1)}, bf16[32,3072]{1,0:T(8,128)(2,1)S(1)}, u32[]{:S(2)}, u32[]{:S(2)}) collective-permute-start(bf16[32,3072]{1,0:T(8,128)(2,1)S(1)} %collective-permute-done.14.refs_6_), channel_id=1, source_target_pairs={{0,2},{1,3},{2,4},{3,5},{4,6},{5,7},{6,8},{7,9},{8,10},{9,11},{10,... | collective-permute-start | bytes 589832 | tf_op jit(solution)/shard_map/ppermute | solution.py:48
  46.9 8.1 %collective-permute-start.13 = (bf16[32,3072]{1,0:T(8,128)(2,1)S(1)}, bf16[32,3072]{1,0:T(8,128)(2,1)S(1)}, u32[]{:S(2)}, u32[]{:S(2)}) collective-permute-start(bf16[32,3072]{1,0:T(8,128)(2,1)S(1)} %collective-permute-done.6.refs_4_), channel_id=1, source_target_pairs={{0,16},{1,17},{2,18},{3,19},{4,20},{5,21},{6,22},{7,23},{8,24},{9,... | collective-permute-start | bytes 589832 | tf_op jit(solution)/shard_map/ppermute | solution.py:52
  47.3 1.7 copy-start.1
  49.0 0.9 copy-start.7
  49.9 5.0 %copy-start.2 = (bf16[1,3072,384]{2,1,0:T(8,128)(2,1)S(1)}, bf16[1,3072,384]{2,1,0:T(8,128)(2,1)}, u32[]{:S(2)}) copy-start(bf16[1,3072,384]{2,1,0:T(8,128)(2,1)} %param.12) | copy-start | bytes 7077892
  51.7 5.2 %collective-permute-start.8 = (bf16[256,384]{1,0:T(8,128)(2,1)S(1)}, bf16[256,384]{1,0:T(8,128)(2,1)S(1)}, u32[]{:S(2)}, u32[]{:S(2)}) collective-permute-start(bf16[256,384]{1,0:T(8,128)(2,1)S(1)} %get-tuple-element.19), channel_id=1, source_target_pairs={{0,1},{1,0},{2,3},{3,2},{4,5},{5,4},{6,7},{7,6},{8,9},{9,8},{10,11... | collective-permute-start | bytes 589832 | tf_op jit(solution)/shard_map/ppermute | solution.py:56
  56.8 4.1 %copy-start.3 = (bf16[1,128,3072]{2,1,0:T(8,128)(2,1)S(1)}, bf16[1,128,3072]{2,1,0:T(8,128)(2,1)}, u32[]{:S(2)}) copy-start(bf16[1,128,3072]{2,1,0:T(8,128)(2,1)} %param.13) | copy-start | bytes 2359300
  56.8 4.1 %copy-start.4 = (bf16[3072,64]{0,1:T(8,128)(2,1)S(1)}, bf16[3072,64]{0,1:T(8,128)(2,1)}, u32[]{:S(2)}) copy-start(bf16[3072,64]{0,1:T(8,128)(2,1)} %param.14) | copy-start | bytes 1179652
  56.8 4.1 %copy-start.8 = (f32[1,3072]{1,0:T(1,128)S(1)}, f32[1,3072]{1,0:T(1,128)}, u32[]{:S(2)}) copy-start(f32[1,3072]{1,0:T(1,128)} %get-tuple-element.16.gate_ref) | copy-start | bytes 36868
  56.8 1.5 collective-permute-start.17
  58.4 9.9 %collective-permute-start.18 = (bf16[1024,128]{1,0:T(8,128)(2,1)S(1)}, bf16[1024,128]{1,0:T(8,128)(2,1)S(1)}, u32[]{:S(2)}, u32[]{:S(2)}) collective-permute-start(bf16[1024,128]{1,0:T(8,128)(2,1)S(1)} %slice.153.q_ref.qa_ref), channel_id=1, source_target_pairs={{0,32},{32,0},{64,96},{96,64},{128,160},{160,128},{192,224},{224,1... | collective-permute-start | bytes 786440 | tf_op jit(solution)/shard_map/ppermute | solution.py:64
  60.9 26.2 %copy-start.9 = (s32[8]{0:T(128)S(1)}, s32[8]{0:T(128)}, u32[]{:S(2)}) copy-start(s32[8]{0:T(128)} %order_ref.3) | copy-start | bytes 100
  66.8 20.3 %copy-start.6 = (bf16[32,32,64]{2,1,0:T(8,128)(2,1)}, bf16[32,32,64]{2,1,0:T(8,128)(2,1)S(1)}, u32[]{:S(2)}) copy-start(bf16[32,32,64]{2,1,0:T(8,128)(2,1)S(1)} %self_attention.1) | copy-start | bytes 393220
  68.3 18.8 %collective-permute-start.24 = (bf16[128,3072]{1,0:T(8,128)(2,1)S(1)}, bf16[128,3072]{1,0:T(8,128)(2,1)S(1)}, u32[]{:S(2)}, u32[]{:S(2)}) collective-permute-start(bf16[128,3072]{1,0:T(8,128)(2,1)S(1)} %bitcast.43), channel_id=1, source_target_pairs={{0,16},{1,17},{2,18},{3,19},{4,20},{5,21},{6,22},{7,23},{8,24},{9,... | collective-permute-start | bytes 2359304 | tf_op jit(solution)/shard_map/ppermute | solution.py:52
  68.8 12.9 %collective-permute-start.19 = (bf16[1024,256]{1,0:T(8,128)(2,1)S(1)}, bf16[1024,256]{1,0:T(8,128)(2,1)S(1)}, u32[]{:S(2)}, u32[]{:S(2)}) collective-permute-start(bf16[1024,256]{1,0:T(8,128)(2,1)S(1)} %slice.154.kv_ref.refs_0_), channel_id=1, source_target_pairs={{0,64},{32,96},{64,128},{96,160},{128,192},{160,224},{192,0},{224,... | collective-permute-start | bytes 1572872 | tf_op jit(solution)/shard_map/ppermute | solution.py:60
  70.3 13.0 %collective-permute-start.20 = (bf16[1024,256]{1,0:T(8,128)(2,1)S(1)}, bf16[1024,256]{1,0:T(8,128)(2,1)S(1)}, u32[]{:S(2)}, u32[]{:S(2)}) collective-permute-start(bf16[1024,256]{1,0:T(8,128)(2,1)S(1)} %slice.154.kv_ref.refs_0_), channel_id=1, source_target_pairs={{0,192},{32,224},{64,0},{96,32},{128,64},{160,96},{192,128},{224,1... | collective-permute-start | bytes 1572872 | tf_op jit(solution)/shard_map/ppermute | solution.py:60
  70.8 28.9 %collective-permute-start.23 = (bf16[128,3072]{1,0:T(8,128)(2,1)S(1)}, bf16[128,3072]{1,0:T(8,128)(2,1)S(1)}, u32[]{:S(2)}, u32[]{:S(2)}) collective-permute-start(bf16[128,3072]{1,0:T(8,128)(2,1)S(1)} %bitcast.44), channel_id=1, source_target_pairs={{0,1},{1,0},{2,3},{3,2},{4,5},{5,4},{6,7},{7,6},{8,9},{9,8},{10,11... | collective-permute-start | bytes 2359304 | tf_op jit(solution)/shard_map/ppermute | solution.py:56
  81.7 11.9 %collective-permute-start.21 = (bf16[512,256]{1,0:T(8,128)(2,1)S(1)}, bf16[512,256]{1,0:T(8,128)(2,1)S(1)}, u32[]{:S(2)}, u32[]{:S(2)}) collective-permute-start(bf16[512,256]{1,0:T(8,128)(2,1)S(1)} %slice.155), channel_id=1, source_target_pairs={{0,64},{32,96},{64,128},{96,160},{128,192},{160,224},{192,0},{224,... | collective-permute-start | bytes 786440 | tf_op jit(solution)/shard_map/ppermute | solution.py:60
  83.3 10.3 %collective-permute-start.22 = (bf16[512,256]{1,0:T(8,128)(2,1)S(1)}, bf16[512,256]{1,0:T(8,128)(2,1)S(1)}, u32[]{:S(2)}, u32[]{:S(2)}) collective-permute-start(bf16[512,256]{1,0:T(8,128)(2,1)S(1)} %slice.156), channel_id=1, source_target_pairs={{0,192},{32,224},{64,0},{96,32},{128,64},{160,96},{192,128},{224,1... | collective-permute-start | bytes 786440 | tf_op jit(solution)/shard_map/ppermute | solution.py:60
  87.1 21.9 %collective-permute-start.25 = (bf16[128,3072]{1,0:T(8,128)(2,1)S(1)}, bf16[128,3072]{1,0:T(8,128)(2,1)}, u32[]{:S(2)}, u32[]{:S(2)}) collective-permute-start(bf16[128,3072]{1,0:T(8,128)(2,1)S(1)} %collective-permute-done.24.w2_ref), channel_id=1, source_target_pairs={{0,1},{1,0},{2,3},{3,2},{4,5},{5,4},{6,7},{7,6},{8,9},{9,8},{10,11... | collective-permute-start | bytes 2359304 | tf_op jit(solution)/shard_map/ppermute | solution.py:56
  95.0 0.8 copy-start.5
  95.8 13.2 %all-to-all-start = ((bf16[8,272,128]{2,1,0:T(8,128)(2,1)}), bf16[8,272,128]{2,1,0:T(8,128)(2,1)S(1)}, u32[]{:S(2)}, u32[]{:S(2)}) async-start(bf16[8,272,128]{2,1,0:T(8,128)(2,1)} %copy-done.5), calls=%async_computation | async-start | bytes 1114112 | tf_op jit(solution)/shard_map/all_to_all | solution.py:493
  99.7 72.9 %reduce-scatter.2.cloned.1.call-start = ((), (), s32[]{:S(2)}) async-start(), calls=%async_computation.5 | async-start | bytes 1769472 | tf_op jit(solution)/shard_map/reduce_scatter | solution.py:498
  114.1 17.2 %copy-start.10 = (bf16[1,32,3072]{2,1,0:T(8,128)(2,1)S(1)}, bf16[1,32,3072]{2,1,0:T(8,128)(2,1)}, u32[]{:S(2)}) copy-start(bf16[1,32,3072]{2,1,0:T(8,128)(2,1)} %param.8) | copy-start | bytes 589828
  132.3 21.8 %all-to-all-start.2 = ((bf16[8,2,1024]{2,1,0:T(2,128)(2,1)}), bf16[8,2,1024]{2,1,0:T(2,128)(2,1)S(1)}, u32[]{:S(2)}, u32[]{:S(2)}) async-start(bf16[8,2,1024]{2,1,0:T(2,128)(2,1)} %reshape.55), calls=%async_computation.3 | async-start | bytes 65536 | tf_op jit(solution)/shard_map/all_to_all | solution.py:508
  155.1 14.8 %all-to-all-start.3 = ((bf16[32,2,1024]{2,1,0:T(2,128)(2,1)}), bf16[32,2,1024]{2,1,0:T(2,128)(2,1)S(1)}, u32[]{:S(2)}, u32[]{:S(2)}) async-start(bf16[32,2,1024]{2,1,0:T(2,128)(2,1)} %reshape.57), calls=%async_computation.4 | async-start | bytes 262144 | tf_op jit(solution)/shard_map/all_to_all | solution.py:512
Sparse Core Ops, SparseCore 0:
  114.3 48.4 reduce-scatter.1
